TPU v7x, 256 devices: a whole 4x4x8 slice. The times are simulated.
256 devices in a mesh: kf: 64 (over z, y, core), head: 4 (over x).
Axes of the slice: x: 4, y: 4, z: 8, core: 2. Of those that a mesh axis runs over, the one named last changes fastest.
Arguments:
- key_states: bfloat16 [128, 510, 1280], P('kf', None, 'head'), may hold values from -6 to 6
- w_query: bfloat16 [1280, 1280], P(None, 'head')
- w_key: bfloat16 [1280, 1280], P(None, 'head')
- w_value: bfloat16 [1280, 1280], P(None, 'head'), may hold values from -0.15625 to 0.15625
- w_out: bfloat16 [1280, 1280], P('head'), may hold values from -0.625 to 0.625
- gain: float32 [1280], replicated, may hold values from 0.1 to 1.9
- bias: float32 [1280], replicated, may hold values from -3 to 3
- src_key: int32 [896, 510, 2], P('kf'), may hold values from 0 to 127, as said below
- src_tok: int32 [896, 510, 2], P('kf'), may hold values from 0 to 509
- weight_num: int32 [896, 510], P('kf'), may hold values from 0 to 16
Outputs:
- key_out: bfloat16 [128, 510, 1280], P('kf', None, 'head')
- blended: bfloat16 [896, 510, 1280], P('kf', None, 'head')
Inputs may be any that keep to these rules, and one draw needn't show every extreme that they name: `src_key`: keyframe k lies at kf index k // 2, non-key frame f at kf index f // 14. The two source keyframes of every token of frame f are the keyframes bracketing it, f // 7 and min(f // 7 + 1, 127), in either order.
All inputs are finite; a program needn't handle non-finite values.
Results may differ from a plain program's by a relative error of at most 0.015.
Values may be sent and summed in bfloat16 or wider, within the bound.
A program may use at most 128 MiB of HBM per device.

v0:
```python
import jax
import jax.numpy as jnp
from jax import lax
from jax.sharding import PartitionSpec as P

HEADS = 20
DEN = 16


def partner(x, axis, stride):
    return lax.ppermute(x, axis, [(i, i ^ 1 << stride) for i in range(lax.axis_size(axis))])


def from_behind(x, axis, by):
    count = lax.axis_size(axis)
    pairs = [(i, i + by) for i in range(count) if 0 <= i + by < count]
    return lax.ppermute(x, axis, pairs)


def normalize(states, gain, bias):
    values = states.astype(jnp.float32)
    center = jnp.mean(values, axis=-1, keepdims=True)
    spread = jnp.mean((values - center) ** 2, axis=-1, keepdims=True)
    return ((values - center) * lax.rsqrt(spread + 1e-05) * gain + bias).astype(jnp.bfloat16)


def project(normed, weight):
    return jnp.dot(normed, weight, preferred_element_type=jnp.float32).astype(jnp.bfloat16)


def head_attention(parts):
    query_h, key_h, value_h = parts
    scale = query_h.shape[1] ** (-0.5)
    scores = jnp.dot(query_h, key_h.T, preferred_element_type=jnp.float32) * scale
    top = jnp.max(scores, axis=-1, keepdims=True)
    expo = jnp.exp(scores - top)
    probs = (expo / jnp.sum(expo, axis=-1, keepdims=True)).astype(jnp.bfloat16)
    return jnp.dot(probs, value_h, preferred_element_type=jnp.float32).astype(jnp.bfloat16)


def body(key_states, w_query, w_key, w_value, w_out, gain, bias, src_key, src_tok, weight_num):
    frames_here, tokens, width = key_states.shape
    full_width = gain.shape[0]
    full = lax.all_gather(key_states, "head", axis=2, tiled=True)
    normed = normalize(full, gain, bias).reshape(frames_here * tokens, full_width)
    query = project(normed, w_query)
    mates = partner(normed, "kf", 0)
    batch_normed = jnp.concatenate([normed, mates], axis=0)
    mates = partner(batch_normed, "kf", 1)
    batch_normed = jnp.concatenate([batch_normed, mates], axis=0)
    keys = project(batch_normed, w_key)
    values = project(batch_normed, w_value)
    heads_here = HEADS // lax.axis_size("head")
    head_size = width // heads_here

    def split(array):
        return array.reshape(array.shape[0], heads_here, head_size).transpose(1, 0, 2)

    attended = lax.map(head_attention, (split(query), split(keys), split(values)))
    attended = attended.transpose(1, 0, 2).reshape(frames_here * tokens, width)
    terms = jnp.dot(attended, w_out, preferred_element_type=jnp.float32)
    mixed = lax.psum_scatter(terms.astype(jnp.bfloat16), "head", scatter_dimension=1, tiled=True)
    key_out = mixed.reshape(frames_here, tokens, width)
    following = from_behind(key_out[:1], "kf", -1)
    window = jnp.concatenate([key_out, following], axis=0).reshape(-1, width)
    first_frame = lax.axis_index("kf") * frames_here
    rows_first = (src_key[..., 0] - first_frame) * tokens + src_tok[..., 0]
    rows_second = (src_key[..., 1] - first_frame) * tokens + src_tok[..., 1]
    first = jnp.take(window, rows_first, axis=0).astype(jnp.float32)
    second = jnp.take(window, rows_second, axis=0).astype(jnp.float32)
    share = weight_num.astype(jnp.float32) / DEN
    blended = (share[..., None] * first + (1.0 - share)[..., None] * second).astype(jnp.bfloat16)
    return (key_out, blended)


def solution(mesh):
    return jax.shard_map(
        body,
        mesh=mesh,
        in_specs=(
            P("kf", None, "head"),
            P(None, "head"),
            P(None, "head"),
            P(None, "head"),
            P("head", None),
            P(),
            P(),
            P("kf", None, None),
            P("kf", None, None),
            P("kf", None),
        ),
        out_specs=(P("kf", None, "head"), P("kf", None, "head")),
        check_vma=False,
    )
```

profile of v0, /device:TPU:1, one launch (start us, length us, event | category | flops | bytes accessed | tf_op | source)
XLA Modules:
  0.0 558.8 jit_solution(8430249956947816254)
XLA Ops:
  7.2 0.0 copy-start
  7.2 0.0 all-gather.2.cloned.1.call-start
  7.2 0.7 all-gather.2.cloned.1.call-update
  7.9 0.0 reduce-scatter.2.cloned.1.call-start
  8.0 43.4 %all-gather.2.cloned.1.call-done = bf16[2,510,1280]{1,2,0:T(8,128)(2,1)} async-done(((bf16[2,510,320]{1,2,0:T(8,128)(2,1)}), bf16[2,510,1280]{1,2,0:T(8,128)(2,1)}) %all-gather.2.cloned.1.call-update) | async-done | bytes 2611216 | tf_op jit(solution)/shard_map/all_gather | solution.py:44
  51.4 2.3 convert_reduce_fusion
  53.8 2.5 fusion.17
  56.3 1.3 fusion.20
  57.5 2.6 copy.20
  60.1 2.3 reshape.59
  62.4 0.8 collective-permute-start
  63.1 4.5 collective-permute-done
  67.7 1.5 copy-done.3
  69.2 3.1 pad_maximum_fusion
  72.2 1.2 collective-permute-start.1
  73.5 3.1 convolution_convert_fusion.3
  76.5 2.3 copy.21
  78.8 107.5 %collective-permute-done.1 = bf16[2040,1280]{1,0:T(8,128)(2,1)} collective-permute-done((bf16[2040,1280]{1,0:T(8,128)(2,1)}, bf16[2040,1280]{1,0:T(8,128)(2,1)}, u32[]{:S(2)}, u32[]{:S(2)}) %collective-permute-start.1) | collective-permute-done | bytes 5222432 | tf_op jit(solution)/shard_map/ppermute | solution.py:11
  186.4 43.9 %concatenate.11 = bf16[4080,1280]{1,0:T(8,128)(2,1)} concatenate(bf16[1020,1280]{1,0:T(8,128)(2,1)S(1)} %reshape.59, bf16[1020,1280]{1,0:T(8,128)(2,1)} %copy-done.3, bf16[2040,1280]{1,0:T(8,128)(2,1)} %collective-permute-done.1), dimensions={0} | concatenate | bytes 20889600 | tf_op jit(solution)/shard_map/concatenate | solution.py:50
  230.3 11.0 %convolution_convert_fusion.1 = bf16[4080,320]{0,1:T(8,128)(2,1)S(1)} fusion(bf16[4080,1280]{1,0:T(8,128)(2,1)} %concatenate.11, bf16[1280,320]{0,1:T(8,128)(2,1)S(1)} %copy-done), kind=kOutput, calls=%fused_computation.26 | convolution fusion | flops 3343641600 | bytes 13875200 | tf_op jit(solution)/shard_map/dot_general | solution.py:28
  241.3 0.0 copy-start.9
  241.3 4.2 copy.22
  245.5 11.0 %convolution_convert_fusion = bf16[4080,320]{0,1:T(8,128)(2,1)S(1)} fusion(bf16[4080,1280]{1,0:T(8,128)(2,1)} %concatenate.11, bf16[1280,320]{0,1:T(8,128)(2,1)S(1)} %copy-done.9), kind=kOutput, calls=%fused_computation.25 | convolution fusion | flops 3343641600 | bytes 13875200 | tf_op jit(solution)/shard_map/dot_general | solution.py:28
  256.5 0.0 copy-start.11
  256.5 4.2 copy.23
  260.8 137.5 %while.10 = (s32[]{:T(128)}, bf16[5,1020,64]{1,2,0:T(8,128)(2,1)S(1)}, bf16[5,1020,64]{2,1,0:T(8,128)(2,1)}, bf16[5,4080,64]{2,1,0:T(8,128)(2,1)}, bf16[5,4080,64]{2,1,0:T(8,128)(2,1)}, /*index=5*/s32[]{:T(128)}) while((s32[]{:T(128)}, bf16[5,1020,64]{1,2,0:T(8,128)(2,1)S(1)}, bf16[5,1020,64]{2,1,0:T(8,128)(2,1)}, ...), condition=%wide.region_5.6_spmd, body=%wide.region_2.5_spmd.sunk | while | flops 1102887168 | bytes 52509204 | solution.py:59
  260.8 9.4 %multiply_reduce_fusion.2 = (f32[1020]{0:T(1024)S(1)}, f32[1020,4080]{0,1:T(8,128)}) fusion(bf16[5,4080,64]{2,1,0:T(8,128)(2,1)} %get-tuple-element.109, s32[]{:T(128)} %get-tuple-element.100, bf16[5,1020,64]{2,1,0:T(8,128)(2,1)} %get-tuple-element.108), kind=kOutput, calls=%fused_computation.4.clone.1 | convolution fusion | flops 541006976 | bytes 17958128 | tf_op jit(solution)/shard_map/while/body/eval_jaxpr/dot_general | solution.py:34
  270.2 8.6 %fusion.39 = f32[1020]{0:T(1024)S(1)} fusion(f32[1020,4080]{0,1:T(8,128)} %get-tuple-element.92, f32[1020]{0:T(1024)S(1)} %get-tuple-element.93), kind=kLoop, calls=%fused_computation.5.clone.1 | loop fusion | flops 12483780 | bytes 16654560 | tf_op jit(solution)/shard_map/while/body/eval_jaxpr/reduce_sum | solution.py:37
  278.8 9.5 %fusion.40 = bf16[5,1020,64]{1,2,0:T(8,128)(2,1)S(1)} fusion(bf16[5,1020,64]{1,2,0:T(8,128)(2,1)S(1)} %get-tuple-element.101, s32[]{:T(128)} %get-tuple-element.100, f32[1020,4080]{0,1:T(8,128)} %get-tuple-element.92, f32[1020]{0:T(1024)S(1)} %fusion.39, f32[1020]{0:T(1024)S(1)} %get-tuple-element.93, bf16[5,4080,64]{2,1,0:T(8,128)(2,1)} %get-tuple-element.110), kind=kOutput, calls=%fused_computation.9.clone.1 | convolution fusion | flops 549396480 | bytes 17896448 | tf_op jit(solution)/shard_map/while/body/eval_jaxpr/dot_general | solution.py:38
  288.3 9.4 %multiply_reduce_fusion.2 = (f32[1020]{0:T(1024)S(1)}, f32[1020,4080]{0,1:T(8,128)}) fusion(bf16[5,4080,64]{2,1,0:T(8,128)(2,1)} %get-tuple-element.109, s32[]{:T(128)} %get-tuple-element.100, bf16[5,1020,64]{2,1,0:T(8,128)(2,1)} %get-tuple-element.108), kind=kOutput, calls=%fused_computation.4.clone.1 | convolution fusion | flops 541006976 | bytes 17958128 | tf_op jit(solution)/shard_map/while/body/eval_jaxpr/dot_general | solution.py:34
  297.7 8.6 %fusion.39 = f32[1020]{0:T(1024)S(1)} fusion(f32[1020,4080]{0,1:T(8,128)} %get-tuple-element.92, f32[1020]{0:T(1024)S(1)} %get-tuple-element.93), kind=kLoop, calls=%fused_computation.5.clone.1 | loop fusion | flops 12483780 | bytes 16654560 | tf_op jit(solution)/shard_map/while/body/eval_jaxpr/reduce_sum | solution.py:37
  306.3 9.5 %fusion.40 = bf16[5,1020,64]{1,2,0:T(8,128)(2,1)S(1)} fusion(bf16[5,1020,64]{1,2,0:T(8,128)(2,1)S(1)} %get-tuple-element.101, s32[]{:T(128)} %get-tuple-element.100, f32[1020,4080]{0,1:T(8,128)} %get-tuple-element.92, f32[1020]{0:T(1024)S(1)} %fusion.39, f32[1020]{0:T(1024)S(1)} %get-tuple-element.93, bf16[5,4080,64]{2,1,0:T(8,128)(2,1)} %get-tuple-element.110), kind=kOutput, calls=%fused_computation.9.clone.1 | convolution fusion | flops 549396480 | bytes 17896448 | tf_op jit(solution)/shard_map/while/body/eval_jaxpr/dot_general | solution.py:38
  315.8 9.4 %multiply_reduce_fusion.2 = (f32[1020]{0:T(1024)S(1)}, f32[1020,4080]{0,1:T(8,128)}) fusion(bf16[5,4080,64]{2,1,0:T(8,128)(2,1)} %get-tuple-element.109, s32[]{:T(128)} %get-tuple-element.100, bf16[5,1020,64]{2,1,0:T(8,128)(2,1)} %get-tuple-element.108), kind=kOutput, calls=%fused_computation.4.clone.1 | convolution fusion | flops 541006976 | bytes 17958128 | tf_op jit(solution)/shard_map/while/body/eval_jaxpr/dot_general | solution.py:34
  325.2 8.6 %fusion.39 = f32[1020]{0:T(1024)S(1)} fusion(f32[1020,4080]{0,1:T(8,128)} %get-tuple-element.92, f32[1020]{0:T(1024)S(1)} %get-tuple-element.93), kind=kLoop, calls=%fused_computation.5.clone.1 | loop fusion | flops 12483780 | bytes 16654560 | tf_op jit(solution)/shard_map/while/body/eval_jaxpr/reduce_sum | solution.py:37
  333.7 9.5 %fusion.40 = bf16[5,1020,64]{1,2,0:T(8,128)(2,1)S(1)} fusion(bf16[5,1020,64]{1,2,0:T(8,128)(2,1)S(1)} %get-tuple-element.101, s32[]{:T(128)} %get-tuple-element.100, f32[1020,4080]{0,1:T(8,128)} %get-tuple-element.92, f32[1020]{0:T(1024)S(1)} %fusion.39, f32[1020]{0:T(1024)S(1)} %get-tuple-element.93, bf16[5,4080,64]{2,1,0:T(8,128)(2,1)} %get-tuple-element.110), kind=kOutput, calls=%fused_computation.9.clone.1 | convolution fusion | flops 549396480 | bytes 17896448 | tf_op jit(solution)/shard_map/while/body/eval_jaxpr/dot_general | solution.py:38
  343.3 9.4 %multiply_reduce_fusion.2 = (f32[1020]{0:T(1024)S(1)}, f32[1020,4080]{0,1:T(8,128)}) fusion(bf16[5,4080,64]{2,1,0:T(8,128)(2,1)} %get-tuple-element.109, s32[]{:T(128)} %get-tuple-element.100, bf16[5,1020,64]{2,1,0:T(8,128)(2,1)} %get-tuple-element.108), kind=kOutput, calls=%fused_computation.4.clone.1 | convolution fusion | flops 541006976 | bytes 17958128 | tf_op jit(solution)/shard_map/while/body/eval_jaxpr/dot_general | solution.py:34
  352.6 8.6 %fusion.39 = f32[1020]{0:T(1024)S(1)} fusion(f32[1020,4080]{0,1:T(8,128)} %get-tuple-element.92, f32[1020]{0:T(1024)S(1)} %get-tuple-element.93), kind=kLoop, calls=%fused_computation.5.clone.1 | loop fusion | flops 12483780 | bytes 16654560 | tf_op jit(solution)/shard_map/while/body/eval_jaxpr/reduce_sum | solution.py:37
  361.2 9.5 %fusion.40 = bf16[5,1020,64]{1,2,0:T(8,128)(2,1)S(1)} fusion(bf16[5,1020,64]{1,2,0:T(8,128)(2,1)S(1)} %get-tuple-element.101, s32[]{:T(128)} %get-tuple-element.100, f32[1020,4080]{0,1:T(8,128)} %get-tuple-element.92, f32[1020]{0:T(1024)S(1)} %fusion.39, f32[1020]{0:T(1024)S(1)} %get-tuple-element.93, bf16[5,4080,64]{2,1,0:T(8,128)(2,1)} %get-tuple-element.110), kind=kOutput, calls=%fused_computation.9.clone.1 | convolution fusion | flops 549396480 | bytes 17896448 | tf_op jit(solution)/shard_map/while/body/eval_jaxpr/dot_general | solution.py:38
  370.8 9.4 %multiply_reduce_fusion.2 = (f32[1020]{0:T(1024)S(1)}, f32[1020,4080]{0,1:T(8,128)}) fusion(bf16[5,4080,64]{2,1,0:T(8,128)(2,1)} %get-tuple-element.109, s32[]{:T(128)} %get-tuple-element.100, bf16[5,1020,64]{2,1,0:T(8,128)(2,1)} %get-tuple-element.108), kind=kOutput, calls=%fused_computation.4.clone.1 | convolution fusion | flops 541006976 | bytes 17958128 | tf_op jit(solution)/shard_map/while/body/eval_jaxpr/dot_general | solution.py:34
  380.1 8.6 %fusion.39 = f32[1020]{0:T(1024)S(1)} fusion(f32[1020,4080]{0,1:T(8,128)} %get-tuple-element.92, f32[1020]{0:T(1024)S(1)} %get-tuple-element.93), kind=kLoop, calls=%fused_computation.5.clone.1 | loop fusion | flops 12483780 | bytes 16654560 | tf_op jit(solution)/shard_map/while/body/eval_jaxpr/reduce_sum | solution.py:37
  388.7 9.5 %fusion.40 = bf16[5,1020,64]{1,2,0:T(8,128)(2,1)S(1)} fusion(bf16[5,1020,64]{1,2,0:T(8,128)(2,1)S(1)} %get-tuple-element.101, s32[]{:T(128)} %get-tuple-element.100, f32[1020,4080]{0,1:T(8,128)} %get-tuple-element.92, f32[1020]{0:T(1024)S(1)} %fusion.39, f32[1020]{0:T(1024)S(1)} %get-tuple-element.93, bf16[5,4080,64]{2,1,0:T(8,128)(2,1)} %get-tuple-element.110), kind=kOutput, calls=%fused_computation.9.clone.1 | convolution fusion | flops 549396480 | bytes 17896448 | tf_op jit(solution)/shard_map/while/body/eval_jaxpr/dot_general | solution.py:38
  398.3 0.8 copy-done.12
  399.1 4.2 convolution_convert_fusion.2
  403.3 0.0 reduce-scatter.2.cloned.1.call-update
  403.5 0.1 reshape.86
  403.6 0.1 reshape.90
  403.7 37.0 %reduce-scatter.2.cloned.1.call-done = bf16[1020,320]{0,1:T(8,128)(2,1)} async-done(((bf16[1020,1280]{0,1:T(8,128)(2,1)}), bf16[1020,320]{0,1:T(8,128)(2,1)}) %reduce-scatter.2.cloned.1.call-update) | async-done | bytes 652816 | tf_op jit(solution)/shard_map/reduce_scatter | solution.py:62
  440.7 1.0 slice_bitcast_fusion
  441.7 2.5 collective-permute-start.2
  444.2 3.1 reshape.64
  447.3 0.8 copy.26
  448.2 0.9 copy.32
  449.1 1.0 collective-permute-done.2
  450.0 0.2 copy.27
  450.3 0.2 pad_maximum_fusion.1
  450.5 0.5 reshape.65
  451.0 29.1 %gather_fusion = bf16[7140,320]{1,0:T(8,128)(2,1)} fusion(bf16[1530,320]{1,0:T(8,128)(2,1)S(1)} %reshape.65, s32[7168]{0:T(1024)S(1)} %pad_clamp_fusion.1), kind=kCustom, calls=%fused_computation.clone | custom fusion | bytes 9167760 | tf_op jit(solution)/shard_map/jit(_take)/gather | solution.py:69
  480.2 6.9 %reshape.94 = bf16[14,510,320]{2,1,0:T(8,128)(2,1)} reshape(bf16[7140,320]{1,0:T(8,128)(2,1)} %gather_fusion) | data formatting | bytes 9139200 | tf_op jit(solution)/shard_map/jit(_take)/gather | solution.py:69
  487.1 8.6 %copy.34 = bf16[14,510,320]{1,0,2:T(8,128)(2,1)} copy(bf16[14,510,320]{2,1,0:T(8,128)(2,1)} %reshape.94) | data formatting | bytes 9139200 | tf_op jit(solution)/shard_map/jit(_take)/gather | solution.py:69
  495.7 29.1 %gather_fusion.1 = bf16[7140,320]{1,0:T(8,128)(2,1)} fusion(bf16[1530,320]{1,0:T(8,128)(2,1)S(1)} %reshape.65, s32[7168]{0:T(1024)S(1)} %pad_clamp_fusion), kind=kCustom, calls=%fused_computation.1.clone | custom fusion | bytes 9167760 | tf_op jit(solution)/shard_map/jit(_take)/gather | solution.py:70
  524.8 6.9 %reshape.95 = bf16[14,510,320]{2,1,0:T(8,128)(2,1)} reshape(bf16[7140,320]{1,0:T(8,128)(2,1)} %gather_fusion.1) | data formatting | bytes 9139200 | tf_op jit(solution)/shard_map/jit(_take)/gather | solution.py:70
  531.7 8.6 %copy.35 = bf16[14,510,320]{1,0,2:T(8,128)(2,1)} copy(bf16[14,510,320]{2,1,0:T(8,128)(2,1)} %reshape.95) | data formatting | bytes 9139200 | tf_op jit(solution)/shard_map/jit(_take)/gather | solution.py:70
  540.3 6.9 %add_convert_fusion = bf16[14,510,320]{1,0,2:T(8,128)(2,1)S(1)} fusion(bf16[14,510,320]{1,0,2:T(8,128)(2,1)} %copy.35, bf16[14,510,320]{1,0,2:T(8,128)(2,1)} %copy.34, f32[14,510]{1,0:T(8,128)S(1)} %get-tuple-element.56, f32[14,510]{1,0:T(8,128)S(1)} %get-tuple-element.55, pred[14,510]{1,0:T(8,128)(4,1)S(1)} %get-tuple-element.47, ...), kind=kLoop, calls=%fused_computation.20 | loop fusion | flops 18278400 | bytes 13780200 | tf_op jit(solution)/shard_map/convert_element_type | solution.py:72
  547.2 4.7 copy.33
  (30 shorter events, 0.2 us)
Async XLA Ops:
  7.2 223.2 %copy-start = (bf16[1280,320]{0,1:T(8,128)(2,1)S(1)}, bf16[1280,320]{0,1:T(8,128)(2,1)}, u32[]{:S(2)}) copy-start(bf16[1280,320]{0,1:T(8,128)(2,1)} %param.16) | copy-start | bytes 2457604
  7.2 49.1 %copy-start.8 = (f32[1280]{0:T(1024)S(1)}, f32[1280]{0:T(1024)}, u32[]{:S(2)}) copy-start(f32[1280]{0:T(1024)} %param.19) | copy-start | bytes 15364
  7.2 49.1 %copy-start.7 = (f32[1280]{0:T(1024)S(1)}, f32[1280]{0:T(1024)}, u32[]{:S(2)}) copy-start(f32[1280]{0:T(1024)} %param.20) | copy-start | bytes 15364
  7.2 44.2 %all-gather.2.cloned.1.call-start = ((), (), s32[]{:S(2)}) async-start(), calls=%async_computation.1 | async-start | bytes 3276800 | tf_op jit(solution)/shard_map/all_gather | solution.py:44
  7.9 432.7 %reduce-scatter.2.cloned.1.call-start = ((), (), s32[]{:S(2)}) async-start(), calls=%async_computation.2 | async-start | bytes 3276800 | tf_op jit(solution)/shard_map/reduce_scatter | solution.py:62
  51.4 4.9 copy-start.2
  62.4 5.3 collective-permute-start
  67.7 1.5 copy-start.3
  72.2 114.1 %collective-permute-start.1 = (bf16[2040,1280]{1,0:T(8,128)(2,1)}, bf16[2040,1280]{1,0:T(8,128)(2,1)}, u32[]{:S(2)}, u32[]{:S(2)}) collective-permute-start(bf16[2040,1280]{1,0:T(8,128)(2,1)} %pad_maximum_fusion), channel_id=1, source_target_pairs={{0,8},{4,12},{8,0},{12,4},{16,24},{20,28},{24,16},{28,20},{32,40},... | collective-permute-start | bytes 15667208 | tf_op jit(solution)/shard_map/ppermute | solution.py:11
  241.3 4.2 copy-start.9
  256.5 4.2 copy-start.11
  260.8 138.3 %copy-start.10 = (bf16[320,1280]{1,0:T(8,128)(2,1)S(1)}, bf16[320,1280]{1,0:T(8,128)(2,1)}, u32[]{:S(2)}) copy-start(bf16[320,1280]{1,0:T(8,128)(2,1)} %param.18) | copy-start | bytes 2457604
  398.2 0.8 copy-start.12
  399.1 4.2 copy-start.4
  399.1 4.3 copy-start.5
  399.1 45.1 %copy-start.6 = (s32[14,510]{1,0:T(8,128)S(1)}, s32[14,510]{1,0:T(8,128)}, u32[]{:S(2)}) copy-start(s32[14,510]{1,0:T(8,128)} %param.23) | copy-start | bytes 85684
  441.7 8.4 %collective-permute-start.2 = (bf16[1,510,320]{1,2,0:T(8,128)(2,1)S(1)}, bf16[1,510,320]{1,2,0:T(8,128)(2,1)S(1)}, u32[]{:S(2)}, u32[]{:S(2)}) collective-permute-start(bf16[1,510,320]{1,2,0:T(8,128)(2,1)S(1)} %slice_bitcast_fusion), channel_id=1, source_target_pairs={{4,0},{8,4},{12,8},{16,12},{20,16},{24,20},{28,24},{32,28},{36,32}... | collective-permute-start | bytes 979208 | tf_op jit(solution)/shard_map/ppermute | solution.py:17
  540.3 11.6 %copy-start.1 = (bf16[1280,320]{0,1:T(8,128)(2,1)S(1)}, bf16[1280,320]{0,1:T(8,128)(2,1)}, u32[]{:S(2)}) copy-start(bf16[1280,320]{0,1:T(8,128)(2,1)} %param.16) | copy-start | bytes 2457604
Sparse Core Ops, SparseCore 0:
  9.8 41.5 all-gather.1
  403.4 37.2 reduce-scatter.1
where the time goes:
time: 562 us; the launch traced here: 559 us
  waiting for transfers between devices  194 us (35%)
  local copies, waits for them, and re-layouts  163 us (29%)
  matrix products  124 us (22%)
  other arithmetic  59.3 us (11%)
  between operations  14.3 us (3%)
    ppermute x2, waiting for transfers between devices, partner(): lax.ppermute(x, axis, [(i, i ^ 1 << stride) for i in range(lax.axis_size(...  112 us
    dot_general x5, matrix products, head_attention(): jnp.dot(probs, value_h, preferred_element_type=jnp.float32)  47.7 us
    dot_general x5, matrix products, head_attention(): jnp.dot(query_h, key_h.T, preferred_element_type=jnp.float32) * scale  46.9 us
    gather x3, local copies, waits for them, and re-layouts, body(): second = jnp.take(window, rows_second, axis=0).astype(jnp.float32)  44.6 us
    gather x3, local copies, waits for them, and re-layouts, body(): first = jnp.take(window, rows_first, axis=0).astype(jnp.float32)  44.6 us
    concatenate x1, local copies, waits for them, and re-layouts, body(): batch_normed = jnp.concatenate([batch_normed, mates], axis=0)  43.9 us
    all_gather x1, waiting for transfers between devices, body(): full = lax.all_gather(key_states, 'head', axis=2, tiled=True)  43.4 us
    reduce_sum x5, other arithmetic, head_attention(): probs = (expo / jnp.sum(expo, axis=-1, keepdims=True)).astype(jnp.bfloat16)  42.9 us
  transfers between devices with their start and end apart: 5, of which 5 were waited for; matrix products, arithmetic and copies ran while one was open for 2% of the time, Pallas kernels for 0%

commit v1 on v0

v1 whole, which is shorter than its diff:
```python
import functools

import jax
import jax.numpy as jnp
from jax import lax
from jax.experimental import pallas as pl
from jax.experimental.pallas import tpu as pltpu
from jax.sharding import PartitionSpec as P

MESH = pl.DeviceIdType.MESH
HD = 64
DEN = 16
TOK = 510
PAD = 512
QW = 2 * PAD
SCORE_SCALE = 0.125 * 1.4426950408889634
LOWEST = -3e38


def attend(n_x, x_ref, wq_hbm, wk_hbm, wv_hbm, wo_hbm, gain_ref, bias_ref, out_ref,
           wq, wk, wv, wo, xg, nt, qz, kb, vb, ones, acc, top, at, wt, wog, gb,
           w_sem, x_send, x_recv, kv_send, kv_recv, a_send, a_recv, o_send, o_recv):
    kf = lax.axis_index("kf")
    x = lax.axis_index("head")
    right, left, far = lax.rem(x + 1, n_x), lax.rem(x + 3, n_x), lax.rem(x + 2, n_x)
    core = kf + 1 - 2 * lax.rem(kf, 2)
    ymate = kf + 2 - 4 * lax.rem(kf // 2, 2)
    dev_r, dev_l, dev_far, dev_core, dev_y = (kf, right), (kf, left), (kf, far), (core, x), (ymate, x)
    width = x_ref.shape[1]

    def copy(src, dst, send, recv, dev):
        return pltpu.make_async_remote_copy(
            src_ref=src, dst_ref=dst, send_sem=send, recv_sem=recv, device_id=dev, device_id_type=MESH)

    barrier = pltpu.get_barrier_semaphore()
    for dev in (dev_r, dev_l, dev_far, dev_core, dev_y):
        pl.semaphore_signal(barrier, inc=1, device_id=dev, device_id_type=MESH)

    loads = [pltpu.make_async_copy(a, b, w_sem.at[i])
             for i, (a, b) in enumerate(((wq_hbm, wq), (wk_hbm, wk), (wv_hbm, wv), (wo_hbm, wo)))]
    for load in loads:
        load.start()

    def xrow(owner, half=None):
        if half is None:
            return pl.ds(pl.multiple_of(owner * width, 64), width)
        return pl.ds(pl.multiple_of(owner * width + half * (width // 2), 32), width // 2)

    for f in range(2):
        xg[f, xrow(x), pl.ds(PAD - 128, 128)] = jnp.zeros((width, 128), jnp.bfloat16)
        xg[f, xrow(x), pl.ds(0, TOK)] = x_ref[f]
    pl.semaphore_wait(barrier, 5)

    def x_own(f):
        piece = xg.at[f, xrow(x)]
        return (copy(piece, piece, x_send.at[f, 0], x_recv.at[f, 0], dev_r),
                copy(piece, piece, x_send.at[f, 1], x_recv.at[f, 1], dev_l))

    def x_fwd(f):
        a, b = xg.at[f, xrow(left, 0)], xg.at[f, xrow(right, 1)]
        return (copy(a, a, x_send.at[f, 2], x_recv.at[f, 2], dev_r),
                copy(b, b, x_send.at[f, 3], x_recv.at[f, 3], dev_l))

    def x_arrive(f):
        a, b = xg.at[f, xrow(left)], xg.at[f, xrow(right)]
        copy(a, a, x_send.at[f, 0], x_recv.at[f, 0], dev_l).wait_recv()
        x_fwd(f)[0].start()
        copy(b, b, x_send.at[f, 1], x_recv.at[f, 1], dev_r).wait_recv()
        x_fwd(f)[1].start()

    def x_last(f):
        a, b = xg.at[f, xrow(far, 0)], xg.at[f, xrow(far, 1)]
        copy(a, a, x_send.at[f, 2], x_recv.at[f, 2], dev_l).wait_recv()
        copy(b, b, x_send.at[f, 3], x_recv.at[f, 3], dev_r).wait_recv()

    for c in x_own(0):
        c.start()

    gb[...] = jnp.concatenate([jnp.broadcast_to(gain_ref[...], (8, gain_ref.shape[1])).T[:, 0:1],
                               jnp.broadcast_to(bias_ref[...], (8, bias_ref.shape[1])).T[:, 0:1]], axis=1)
    qz[...] = jnp.zeros_like(qz)
    row = lax.broadcasted_iota(jnp.int32, (16, QW), 0)
    col = lax.broadcasted_iota(jnp.int32, (16, QW), 1)
    ones[0] = jnp.where((row == 0) & (col % PAD < TOK), 1.0, 0.0).astype(jnp.bfloat16)
    ones[1] = jnp.where((row == 0) & ((col < PAD) | (col % 256 < 254)), 1.0, 0.0).astype(jnp.bfloat16)
    loads[3].wait()
    for j in range(n_x):
        part = wo[:, j * width:(j + 1) * width].astype(jnp.float32)
        wt[j] = part.T.astype(jnp.bfloat16)
    wog[x] = wt[x]

    x_arrive(0)
    for c in x_own(1):
        c.start()
    for load in loads[:3]:
        load.wait()

    def project(f):
        def norm(i, _):
            cols = pl.ds(pl.multiple_of(i * 128, 128), 128)
            values = xg[f, :, cols].astype(jnp.float32)
            center = jnp.mean(values, axis=0, keepdims=True)
            off = values - center
            spread = jnp.mean(off * off, axis=0, keepdims=True)
            nt[:, cols] = (off * lax.rsqrt(spread + 1e-05) * gb[:, 0:1] + gb[:, 1:2]).astype(jnp.bfloat16)
            return 0

        lax.fori_loop(0, PAD // 128, norm, 0)
        here = pl.ds(f * PAD, PAD)
        lane = lax.broadcasted_iota(jnp.int32, (width, PAD), 1)
        k = jnp.dot(wk[...], nt[...], preferred_element_type=jnp.float32)
        k = jnp.where(lane < TOK, k, k[:, TOK - 1:TOK]).T.astype(jnp.bfloat16)
        kb[0, f, 0:512, :] = k[:, 0:128]
        kb[0, f, 512:1024, :] = k[:, 128:256]
        kb[0, f, 1024:1280, :] = jnp.concatenate([k[0:256, 256:320], k[256:512, 256:320]], axis=1)
        v = jnp.dot(wv[...], nt[...], preferred_element_type=jnp.float32)
        vb[0, f] = jnp.where(lane < TOK, v, 0.0).astype(jnp.bfloat16)
        for part in pieces(f):
            for c in kv_copies(f, part, 0):
                c.start()
            for c in kv_copies(f, part, 1):
                c.start()
        q = (jnp.dot(wq[...], nt[...], preferred_element_type=jnp.float32) * SCORE_SCALE).astype(jnp.bfloat16)
        for h in range(5):
            half = (h % 2) * HD
            qz[h, half:half + HD, here] = q[h * HD:(h + 1) * HD]
        qz[5, HD:2 * HD, here] = q[4 * HD:5 * HD]

    def pieces(f):
        return (3,) if f == 0 else (0, 1, 2)

    def kv_rows(part):
        if isinstance(part, int):
            return ((pl.ds(0, 1280), pl.ds(0, 320)) if part == 3 else
                    (pl.ds(1024, 256), pl.ds(256, 64)) if part == 2 else
                    (pl.ds(part * 512, 512), pl.ds(part * 128, 128)))
        return pl.ds(pl.multiple_of(part * 512, 512), 512), pl.ds(pl.multiple_of(part * 128, 128), 128)

    def kv_copies(f, part, route, landed=False):
        k_rows, v_rows = kv_rows(part)
        source, target = (0, 0, 2)[route], (1, 2, 3)[route]
        source = target if landed else source
        dev = dev_y if route == 1 else dev_core
        return (copy(kb.at[source, f, k_rows], kb.at[target, f, k_rows],
                     kv_send.at[route, part, 0], kv_recv.at[route, part, 0], dev),
                copy(vb.at[source, f, v_rows], vb.at[target, f, v_rows],
                     kv_send.at[route, part, 1], kv_recv.at[route, part, 1], dev))

    def kv_wait(f, part, route):
        for c in kv_copies(f, part, route, landed=True):
            c.wait_recv()

    def kv_forward(f, part):
        kv_wait(f, part, 1)
        for c in kv_copies(f, part, 2):
            c.start()

    def update(h, s, values, first):
        m0 = jnp.full((1, QW), LOWEST, jnp.float32) if first else top[h]
        m = jnp.maximum(m0, jnp.max(s, axis=0, keepdims=True))
        p = jnp.exp2(s - m).astype(jnp.bfloat16)
        term = jnp.dot(values, p, preferred_element_type=jnp.float32)
        acc[h] = term if first else acc[h] * jnp.exp2(m0 - m) + term
        top[h] = m

    def block(src, h, first=False):
        rows = pl.ds(pl.multiple_of(h // 2 * 512, 512), 512)
        chans = pl.ds(pl.multiple_of(h * HD, HD), HD)
        keys = jnp.concatenate([kb[src, 0, rows, :], kb[src, 1, rows, :]], axis=0)
        vals = jnp.concatenate([vb[src, 0, chans, :], vb[src, 1, chans, :]], axis=1)
        s = jnp.dot(keys, qz[h], preferred_element_type=jnp.float32)
        update(h, s, jnp.concatenate([vals, ones[0]], axis=0), first)

    def block_last(src, first=False):
        keys = jnp.concatenate([kb[src, 0, 1024:1280, :], kb[src, 1, 1024:1280, :]], axis=0)
        vals = jnp.concatenate([vb[src, 0, 256:320, 0:256], vb[src, 1, 256:320, 0:256],
                                vb[src, 0, 256:320, 256:512], vb[src, 1, 256:320, 256:512]], axis=1)
        s = jnp.concatenate([jnp.dot(keys, qz[4], preferred_element_type=jnp.float32),
                             jnp.dot(keys, qz[5], preferred_element_type=jnp.float32)], axis=0)
        update(4, s, jnp.concatenate([vals, ones[1]], axis=0), first)

    def a_row(h, half=None):
        if half is None:
            return pl.ds(pl.multiple_of(h * HD, HD), HD)
        return pl.ds(pl.multiple_of(h * HD + half * 32, 32), 32)

    def a_own(h):
        piece = at.at[x, a_row(h)]
        return (copy(piece, piece, a_send.at[h, 0], a_recv.at[h, 0], dev_r),
                copy(piece, piece, a_send.at[h, 1], a_recv.at[h, 1], dev_l))

    def a_fwd(h):
        a, b = at.at[left, a_row(h, 0)], at.at[right, a_row(h, 1)]
        return (copy(a, a, a_send.at[h, 2], a_recv.at[h, 2], dev_r),
                copy(b, b, a_send.at[h, 3], a_recv.at[h, 3], dev_l))

    def a_arrive(h):
        a, b = at.at[left, a_row(h)], at.at[right, a_row(h)]
        copy(a, a, a_send.at[h, 0], a_recv.at[h, 0], dev_l).wait_recv()
        a_fwd(h)[0].start()
        copy(b, b, a_send.at[h, 1], a_recv.at[h, 1], dev_r).wait_recv()
        a_fwd(h)[1].start()

    def a_last(h):
        a, b = at.at[far, a_row(h, 0)], at.at[far, a_row(h, 1)]
        copy(a, a, a_send.at[h, 2], a_recv.at[h, 2], dev_l).wait_recv()
        copy(b, b, a_send.at[h, 3], a_recv.at[h, 3], dev_r).wait_recv()

    def finish(h):
        at[x, a_row(h), :] = (acc[h, 0:HD, :] / acc[h, HD:HD + 1, :]).astype(jnp.bfloat16)
        for c in a_own(h):
            c.start()

    x_last(0)
    project(0)
    x_arrive(1)
    x_last(1)
    project(1)

    def o_copies():
        return [copy(wt.at[to], wog.at[x], o_send.at[i], o_recv.at[i], (kf, to))
                for i, to in enumerate((right, far, left))]

    for c in o_copies():
        c.start()

    def own(h, _):
        block(0, h, True)
        return 0

    lax.fori_loop(0, 4, own, 0)
    block_last(0, True)

    kv_forward(0, 3)
    kv_wait(0, 3, 0)

    def pair(p, _):
        kv_forward(1, p)
        kv_wait(1, p, 0)

        def core_block(i, _):
            block(1, 2 * p + i)
            return 0

        lax.fori_loop(0, 2, core_block, 0)

        @pl.when(p == 0)
        def _():
            kv_wait(0, 3, 2)

        kv_wait(1, p, 2)

        def head(i, _):
            h = 2 * p + i

            def far_block(src, _):
                block(src, h)
                return 0

            lax.fori_loop(2, 4, far_block, 0)
            finish(h)

            @pl.when(h > 0)
            def _():
                a_arrive(h - 1)
            return 0

        lax.fori_loop(0, 2, head, 0)
        return 0

    lax.fori_loop(0, 2, pair, 0)
    kv_forward(1, 2)
    kv_wait(1, 2, 0)
    block_last(1)
    kv_wait(1, 2, 2)
    block_last(2)
    a_arrive(3)
    block_last(3)
    finish(4)

    for i, source in enumerate((left, far, right)):
        copy(wog.at[source], wog.at[source], o_send.at[i], o_recv.at[i], (kf, source)).wait_recv()
    for h in range(4):
        a_last(h)
    a_arrive(4)
    total = jnp.zeros((width, QW), jnp.float32)
    for g in range(n_x):
        total = total + jnp.dot(wog[g, :, 0:256], at[g, 0:256, :], preferred_element_type=jnp.float32)
    a_last(4)
    tail_w = jnp.concatenate([wog[g, :, 256:320] for g in range(n_x)], axis=1)
    tail_a = jnp.concatenate([at[g, 256:320, :] for g in range(n_x)], axis=0)
    total = total + jnp.dot(tail_w, tail_a, preferred_element_type=jnp.float32)
    total = total.astype(jnp.bfloat16)
    for f in range(2):
        out_ref[f] = total[:, f * PAD:(f + 1) * PAD]

    for f in range(2):
        for c in x_own(f) + x_fwd(f):
            c.wait_send()
        for part in pieces(f):
            for route in range(3):
                for c in kv_copies(f, part, route):
                    c.wait_send()
    for h in range(5):
        for c in a_own(h) + a_fwd(h):
            c.wait_send()
    for c in o_copies():
        c.wait_send()


def blend(base, ko_ref, next_ref, key_ref, tok_ref, num_ref, *rest):
    out_ref = rest[-1]
    j = pl.program_id(0)
    first_key = 2 * lax.axis_index("kf") + base
    rows = (key_ref[0] - first_key) * PAD + tok_ref[0]
    share = num_ref[pl.ds(base * 7 + j, 1), :].astype(jnp.float32) / DEN
    spot = lax.broadcasted_iota(jnp.int32, (2 * PAD, TOK), 0)
    pick = jnp.where(spot == rows[0:1], share, 0.0) + jnp.where(spot == rows[1:2], 1.0 - share, 0.0)
    window = jnp.concatenate([ko_ref[base], next_ref[0] if base else ko_ref[1]], axis=1)
    mixed = jnp.dot(window, pick.astype(jnp.bfloat16), preferred_element_type=jnp.float32)
    out_ref[0] = mixed.astype(jnp.bfloat16)


def blend_first(*refs):
    ko_ref, key_out = refs[0], refs[-2]

    @pl.when(pl.program_id(0) == 0)
    def _():
        key_out[...] = ko_ref[:, :, 0:TOK]

    blend(0, ko_ref, None, *refs[1:-2], refs[-1])


def body(key_states, w_query, w_key, w_value, w_out, gain, bias, src_key, src_tok, weight_num):
    n_x = lax.axis_size("head")
    frames, tokens, width = key_states.shape
    full = gain.shape[0]
    vmem = pl.BlockSpec(memory_space=pltpu.VMEM)
    anywhere = pl.BlockSpec(memory_space=pl.ANY)
    bf16, f32 = jnp.bfloat16, jnp.float32
    dma = pltpu.SemaphoreType.DMA
    ko = pl.pallas_call(
        functools.partial(attend, n_x),
        out_shape=jax.ShapeDtypeStruct((2, width, PAD), bf16),
        in_specs=[vmem, anywhere, anywhere, anywhere, anywhere, vmem, vmem],
        out_specs=vmem,
        scratch_shapes=[
            pltpu.VMEM((width, full), bf16), pltpu.VMEM((width, full), bf16), pltpu.VMEM((width, full), bf16),
            pltpu.VMEM((width, full), bf16),
            pltpu.VMEM((2, full, PAD), bf16),
            pltpu.VMEM((full, PAD), bf16),
            pltpu.VMEM((6, 128, QW), bf16),
            pltpu.VMEM((4, 2, 1280, 128), bf16),
            pltpu.VMEM((4, 2, width, PAD), bf16),
            pltpu.VMEM((2, 16, QW), bf16),
            pltpu.VMEM((5, 80, QW), f32),
            pltpu.VMEM((5, 1, QW), f32),
            pltpu.VMEM((4, width, QW), bf16),
            pltpu.VMEM((4, width, width), bf16),
            pltpu.VMEM((4, width, width), bf16),
            pltpu.VMEM((full, 2), f32),
            dma((4,)), dma((2, 4)), dma((2, 4)), dma((3, 4, 2)), dma((3, 4, 2)),
            dma((5, 4)), dma((5, 4)), dma((3,)), dma((3,)),
        ],
        compiler_params=pltpu.CompilerParams(
            collective_id=0, has_side_effects=True, vmem_limit_bytes=52 * 2**20),
        name="attend",
    )(key_states.transpose(0, 2, 1), w_query.T, w_key.T, w_value.T, w_out,
      gain.reshape(1, full), bias.reshape(1, full))
    n_kf = lax.axis_size("kf")
    following = lax.ppermute(ko[:1], "kf", [(i, i - 1) for i in range(1, n_kf)])

    keys_t, toks_t = src_key.transpose(0, 2, 1), src_tok.transpose(0, 2, 1)
    out = jax.ShapeDtypeStruct((14, width, TOK), bf16)
    cost = pl.CostEstimate(flops=2 * 7 * 320 * 1024 * 512, bytes_accessed=4_000_000, transcendentals=0)

    def index_spec(base):
        return pl.BlockSpec((1, 2, TOK), lambda j: (j + 7 * base, 0, 0))

    def whole(shape):
        return pl.BlockSpec(shape, lambda j: (0,) * len(shape))

    def out_spec(base):
        return pl.BlockSpec((1, width, TOK), lambda j: (j + 7 * base, 0, 0))

    params = pltpu.CompilerParams(vmem_limit_bytes=40 * 2**20)
    key_out, half_done = pl.pallas_call(
        blend_first,
        grid=(7,),
        out_shape=(jax.ShapeDtypeStruct((2, width, TOK), bf16), out),
        in_specs=[whole((2, width, PAD)), index_spec(0), index_spec(0), whole((14, TOK))],
        out_specs=(whole((2, width, TOK)), out_spec(0)),
        compiler_params=params, cost_estimate=cost, name="blend_first",
    )(ko, keys_t, toks_t, weight_num)
    blended = pl.pallas_call(
        functools.partial(blend, 1),
        grid=(7,),
        out_shape=out,
        in_specs=[whole((2, width, PAD)), whole((1, width, PAD)), index_spec(1), index_spec(1), whole((14, TOK)), anywhere],
        out_specs=out_spec(1),
        input_output_aliases={5: 0},
        compiler_params=params, cost_estimate=cost, name="blend_second",
    )(ko, following, keys_t, toks_t, weight_num, half_done)
    return key_out.transpose(0, 2, 1), blended.transpose(0, 2, 1)


def solution(mesh):
    return jax.shard_map(
        body,
        mesh=mesh,
        in_specs=(
            P("kf", None, "head"),
            P(None, "head"),
            P(None, "head"),
            P(None, "head"),
            P("head", None),
            P(),
            P(),
            P("kf", None, None),
            P("kf", None, None),
            P("kf", None),
        ),
        out_specs=(P("kf", None, "head"), P("kf", None, "head")),
        check_vma=False,
    )
```

time: 562 us -> 100 us (0.18)
  waiting for transfers between devices: 194 us -> 0.01 us
  local copies, waits for them, and re-layouts: 163 us -> 2.53 us
  matrix products: 124 us -> 0 us
  Pallas kernels: 0 us -> 91.4 us
  other arithmetic: 59.3 us -> 0 us
  between operations: 14.3 us -> 0.69 us
    dot_general x14 -> x0, matrix products: 124 us -> none  [the longest x5 47.7 us: head_attention(): jnp.dot(probs, value_h, preferred_element_type=jnp.float32)]
    ppermute x3 -> x1, waiting for transfers between devices: 113 us -> 0.01 us  [body(): following = lax.ppermute(ko[:1], 'kf', [(i, i - 1) for i in range(1, n_kf)])]
    pallas_call x0 -> x3, Pallas kernels: none -> 91.4 us  [the longest x1 80.2 us: body(): pl.pallas_call(functools.partial(attend, n_x), out_shape=jax.ShapeDtypeSt...]
    gather x6 -> x0, local copies, waits for them, and re-layouts: 89.2 us -> none  [the longest x3 44.6 us: body(): second = jnp.take(window, rows_second, axis=0).astype(jnp.float32)]
    reduce_sum x7 -> x0, other arithmetic: 47.7 us -> none  [the longest x5 42.9 us: head_attention(): probs = (expo / jnp.sum(expo, axis=-1, keepdims=True)).astype(jnp.bfloat16)]
    concatenate x1 -> x0, local copies, waits for them, and re-layouts: 43.9 us -> none  [body(): batch_normed = jnp.concatenate([batch_normed, mates], axis=0)]
    all_gather x1 -> x0, waiting for transfers between devices: 43.4 us -> none  [body(): full = lax.all_gather(key_states, 'head', axis=2, tiled=True)]
    reduce_scatter x1 -> x0, waiting for transfers between devices: 37 us -> none  [body(): lax.psum_scatter(terms.astype(jnp.bfloat16), 'head', scatter_dimension=1,...]
  transfers between devices with their start and end apart: 5 -> 1, of which waited for: 5 -> 0; matrix products, arithmetic and copies ran while one was open for 2% -> 0% of each run, Pallas kernels for 0% -> 6%
where the time goes in v1:
time: 100 us; the launch traced here: 98.7 us
  Pallas kernels  91.4 us (91%)
  starting transfers between devices  4.11 us (4%)
  local copies, waits for them, and re-layouts  2.53 us (3%)
    pallas_call x1, Pallas kernels, body(): pl.pallas_call(functools.partial(attend, n_x), out_shape=jax.ShapeDtypeSt...  80.2 us
    pallas_call x1, Pallas kernels, body(): pl.pallas_call(blend_first, grid=(7,), out_shape=(jax.ShapeDtypeStruct((2...  5.65 us
    pallas_call x1, Pallas kernels, body(): pl.pallas_call(functools.partial(blend, 1), grid=(7,), out_shape=out, in_...  5.54 us
    ppermute x1, starting transfers between devices, body(): following = lax.ppermute(ko[:1], 'kf', [(i, i - 1) for i in range(1, n_kf)])  4.11 us
  transfers between devices with their start and end apart: 1, of which 0 were waited for; matrix products, arithmetic and copies ran while one was open for 0% of the time, Pallas kernels for 6%

profile of v1, /device:TPU:1, one launch (start us, length us, event | category | flops | bytes accessed | tf_op | source)
XLA Modules:
  0.0 98.7 jit_solution(9441929201067210732)
XLA Ops:
  0.6 0.0 copy-start.3
  0.6 0.7 reshape.10.gain_ref
  1.3 0.7 reshape.11.bias_ref
  2.0 0.0 copy-start
  2.1 1.1 %copy-done = bf16[2,510,320]{1,2,0:T(8,128)(2,1)S(1)} copy-done((bf16[2,510,320]{1,2,0:T(8,128)(2,1)S(1)}, bf16[2,510,320]{1,2,0:T(8,128)(2,1)}, u32[]{:S(2)}) %copy-start) | copy-done | bytes 652824
  3.1 0.0 copy-start.1
  3.1 0.0 copy-start.2
  3.1 80.2 %attend.1.refs_0_.ko_ref = bf16[2,320,512]{2,1,0:T(8,128)(2,1)S(1)} custom-call(bf16[2,320,510]{2,1,0:T(8,128)(2,1)S(1)} %bitcast.8, bf16[320,1280]{1,0:T(8,128)(2,1)} %bitcast.14, bf16[320,1280]{1,0:T(8,128)(2,1)} %bitcast.15, bf16[320,1280]{1,0:T(8,128)(2,1)} %bitcast.16, bf16[320,1280]{1,0:T(8,128)(2,1)} %wo_hbm.1, f32[1,1280]{1,0:T(1,128)S(1)} %reshape.10.gain_ref, ...), custom_call_target="tpu_custom_call" | custom-call | tf_op jit(solution)/shard_map/attend/pallas_call | solution.py:342
  83.4 4.1 %collective-permute-start = (bf16[1,320,512]{2,1,0:T(8,128)(2,1)S(1)}, bf16[1,320,512]{2,1,0:T(8,128)(2,1)S(1)}, u32[]{:S(2)}, u32[]{:S(2)}) collective-permute-start(bf16[1,320,512]{2,1,0:T(8,128)(2,1)S(1)} %slice.3), channel_id=1, source_target_pairs={{4,0},{8,4},{12,8},{16,12},{20,16},{24,20},{28,24},{32,28},{36,32}... | collective-permute-start | bytes 983048 | tf_op jit(solution)/shard_map/ppermute | solution.py:371
  87.5 0.0 copy-done.3
  87.5 0.0 copy-done.1
  87.5 0.0 copy-done.2
  87.5 5.6 %blend_first.1 = (bf16[2,320,510]{2,1,0:T(8,128)(2,1)}, bf16[14,320,510]{2,1,0:T(8,128)(2,1)}) custom-call(bf16[2,320,512]{2,1,0:T(8,128)(2,1)S(1)} %attend.1.refs_0_.ko_ref, s32[14,2,510]{2,1,0:T(2,128)S(1)} %bitcast.9, s32[14,2,510]{2,1,0:T(2,128)S(1)} %bitcast.11, s32[14,510]{1,0:T(8,128)S(1)} %copy-done.3), custom_call_target="tpu_custom_call" | custom-call | flops 2348810240 | bytes 4000000 | tf_op jit(solution)/shard_map/blend_first/pallas_call | solution.py:387
  93.2 0.0 collective-permute-done.next_ref
  93.2 5.5 %blend_second.1 = bf16[14,320,510]{2,1,0:T(8,128)(2,1)} custom-call(bf16[2,320,512]{2,1,0:T(8,128)(2,1)S(1)} %attend.1.refs_0_.ko_ref, bf16[1,320,512]{2,1,0:T(8,128)(2,1)S(1)} %collective-permute-done.next_ref, s32[14,2,510]{2,1,0:T(2,128)S(1)} %bitcast.10, s32[14,2,510]{2,1,0:T(2,128)S(1)} %bitcast.12, ...), custom_call_target="tpu_custom_call", output_to_operand_aliasing={{}: (5, {})} | custom-call | flops 2348810240 | bytes 4000000 | tf_op jit(solution)/shard_map/blend_second/pallas_call | solution.py:395
  (1 shorter events, 0.0 us)
Async XLA Ops:
  0.6 86.9 %copy-start.3 = (s32[14,510]{1,0:T(8,128)S(1)}, s32[14,510]{1,0:T(8,128)}, u32[]{:S(2)}) copy-start(s32[14,510]{1,0:T(8,128)} %num_ref.1) | copy-start | bytes 85684
  2.0 1.1 %copy-start = (bf16[2,510,320]{1,2,0:T(8,128)(2,1)S(1)}, bf16[2,510,320]{1,2,0:T(8,128)(2,1)}, u32[]{:S(2)}) copy-start(bf16[2,510,320]{1,2,0:T(8,128)(2,1)} %param.10) | copy-start | bytes 1958404
  3.1 84.4 %copy-start.1 = (s32[14,510,2]{1,2,0:T(2,128)S(1)}, s32[14,510,2]{1,2,0:T(2,128)}, u32[]{:S(2)}) copy-start(s32[14,510,2]{1,2,0:T(2,128)} %param.17) | copy-start | bytes 171364
  3.1 84.4 %copy-start.2 = (s32[14,510,2]{1,2,0:T(2,128)S(1)}, s32[14,510,2]{1,2,0:T(2,128)}, u32[]{:S(2)}) copy-start(s32[14,510,2]{1,2,0:T(2,128)} %param.18) | copy-start | bytes 171364
  83.4 9.8 %collective-permute-start = (bf16[1,320,512]{2,1,0:T(8,128)(2,1)S(1)}, bf16[1,320,512]{2,1,0:T(8,128)(2,1)S(1)}, u32[]{:S(2)}, u32[]{:S(2)}) collective-permute-start(bf16[1,320,512]{2,1,0:T(8,128)(2,1)S(1)} %slice.3), channel_id=1, source_target_pairs={{4,0},{8,4},{12,8},{16,12},{20,16},{24,20},{28,24},{32,28},{36,32}... | collective-permute-start | bytes 983048 | tf_op jit(solution)/shard_map/ppermute | solution.py:371

commit v2 on v0

v2 whole, which is shorter than its diff:
```python
import functools

import jax
import jax.numpy as jnp
from jax import lax
from jax.experimental import pallas as pl
from jax.experimental.pallas import tpu as pltpu
from jax.sharding import PartitionSpec as P

MESH = pl.DeviceIdType.MESH
HD = 64
DEN = 16
TOK = 510
PAD = 512
QW = 2 * PAD
SCORE_SCALE = 0.125 * 1.4426950408889634
LOWEST = -3e38


def attend(n_x, x_hbm, wq_hbm, wk_hbm, wv_hbm, wo_hbm, gain_ref, bias_ref, out_ref, first_ref,
           xs, wq, wk, wv, wo, xg, nt, qz, kb, vb, ones, acc, top, at, wt, wog, gb,
           in_sem, x_send, x_recv, kv_send, kv_recv, a_send, a_recv, o_send, o_recv):
    kf = lax.axis_index("kf")
    x = lax.axis_index("head")
    right, left, far = lax.rem(x + 1, n_x), lax.rem(x + 3, n_x), lax.rem(x + 2, n_x)
    core = kf + 1 - 2 * lax.rem(kf, 2)
    ymate = kf + 2 - 4 * lax.rem(kf // 2, 2)
    dev_r, dev_l, dev_far, dev_core, dev_y = (kf, right), (kf, left), (kf, far), (core, x), (ymate, x)
    width = xs.shape[1]
    half_w = width // 2

    def copy(src, dst, send, recv, dev):
        return pltpu.make_async_remote_copy(
            src_ref=src, dst_ref=dst, send_sem=send, recv_sem=recv, device_id=dev, device_id_type=MESH)

    barrier = pltpu.get_barrier_semaphore()
    for dev in (dev_r, dev_l, dev_far, dev_core, dev_y):
        pl.semaphore_signal(barrier, inc=1, device_id=dev, device_id_type=MESH)

    loads = [pltpu.make_async_copy(a, b, in_sem.at[i])
             for i, (a, b) in enumerate(((x_hbm, xs), (wo_hbm, wo), (wk_hbm, wk), (wv_hbm, wv), (wq_hbm, wq)))]
    for load in loads:
        load.start()

    def ring(piece, sends, recvs):
        def one(owner, part, i, dev):
            return copy(piece(owner, part), piece(owner, part), sends(i), recvs(i), dev)

        def begin():
            for part, i in ((0, 0), (1, 1)):
                one(x, part, i, dev_r).start()
                one(x, 1 - part, 2 + i, dev_l).start()

        def relay():
            one(left, 0, 0, dev_l).wait_recv()
            one(left, 0, 4, dev_r).start()
            one(right, 1, 2, dev_r).wait_recv()
            one(right, 1, 5, dev_l).start()

        def near():
            one(left, 1, 1, dev_l).wait_recv()
            one(right, 0, 3, dev_r).wait_recv()

        def last():
            one(far, 0, 4, dev_l).wait_recv()
            one(far, 1, 5, dev_r).wait_recv()

        def drain():
            for part, i in ((0, 0), (1, 1)):
                one(x, part, i, dev_r).wait_send()
                one(x, 1 - part, 2 + i, dev_l).wait_send()
            one(left, 0, 4, dev_r).wait_send()
            one(right, 1, 5, dev_l).wait_send()

        return begin, relay, near, last, drain

    def x_piece(f):
        def piece(owner, part):
            return xg.at[f, pl.ds(pl.multiple_of(owner * width + part * half_w, 32), half_w)]

        return ring(piece, lambda i: x_send.at[f, i], lambda i: x_recv.at[f, i])

    x_begin, x_relay, x_near, x_last, x_drain = zip(x_piece(0), x_piece(1))

    loads[0].wait()
    own_rows = pl.ds(pl.multiple_of(x * width, 64), width)
    for f in range(2):
        xg[f, own_rows, pl.ds(PAD - 128, 128)] = jnp.zeros((width, 128), jnp.bfloat16)
        xg[f, own_rows, pl.ds(0, TOK)] = xs[f]
    pl.semaphore_wait(barrier, 5)
    x_begin[0]()

    n_tiles = gain_ref.shape[0]
    for i, ref in enumerate((gain_ref, bias_ref)):
        turned = jnp.concatenate([ref[...], jnp.zeros((16 - n_tiles, 128), jnp.float32)], axis=0).T
        for tile in range(n_tiles):
            gb[i, tile * 128:(tile + 1) * 128, :] = jnp.broadcast_to(turned[:, tile:tile + 1], (128, 128))
    qz[...] = jnp.zeros_like(qz)
    row = lax.broadcasted_iota(jnp.int32, ones.shape[1:], 0)
    col = lax.broadcasted_iota(jnp.int32, ones.shape[1:], 1)
    ones[0] = jnp.where((row == 0) & (col % PAD < TOK), 1.0, 0.0).astype(jnp.bfloat16)
    ones[1] = jnp.where(row == 0, 1.0, 0.0).astype(jnp.bfloat16)
    ones[2] = jnp.where((row == 0) & (col % 256 < 254), 1.0, 0.0).astype(jnp.bfloat16)
    loads[1].wait()
    for j in range(n_x):
        part = wo[:, j * width:(j + 1) * width].astype(jnp.float32)
        wt[j] = part.T.astype(jnp.bfloat16)
    wog[x] = wt[x]
    for load in loads[2:]:
        load.wait()

    def project(f):
        for i in range(PAD // 128):
            cols = pl.ds(i * 128, 128)
            values = xg[f, :, cols].astype(jnp.float32)
            center = jnp.mean(values, axis=0, keepdims=True)
            off = values - center
            spread = jnp.mean(off * off, axis=0, keepdims=True)
            nt[:, cols] = (off * lax.rsqrt(spread + 1e-05) * gb[0] + gb[1]).astype(jnp.bfloat16)

        lane = lax.broadcasted_iota(jnp.int32, (width, PAD), 1)
        k = jnp.dot(wk[...], nt[...], preferred_element_type=jnp.float32)
        k = jnp.where(lane < TOK, k, k[:, TOK - 1:TOK]).T.astype(jnp.bfloat16)
        kb[0, f, 0:512, :] = k[:, 0:128]
        kb[0, f, 512:1024, :] = k[:, 128:256]
        kb[0, f, 1024:1280, :] = jnp.concatenate([k[0:256, 256:320], k[256:512, 256:320]], axis=1)
        v = jnp.dot(wv[...], nt[...], preferred_element_type=jnp.float32)
        vb[0, f] = jnp.where(lane < TOK, v, 0.0).astype(jnp.bfloat16)
        for part in pieces(f):
            for c in kv_copies(f, part, 0):
                c.start()
        kv_to_y(f, pieces(f)[0])
        q = (jnp.dot(wq[...], nt[...], preferred_element_type=jnp.float32) * SCORE_SCALE).astype(jnp.bfloat16)
        for h in range(5):
            half = (h % 2) * HD
            qz[f, h, half:half + HD, :] = q[h * HD:(h + 1) * HD]
        qz[f, 5, HD:2 * HD, :] = q[4 * HD:5 * HD]

    def pieces(f):
        return (3,) if f == 0 else (0, 1, 2)

    def kv_rows(part):
        if isinstance(part, int):
            return ((pl.ds(0, 1280), pl.ds(0, 320)) if part == 3 else
                    (pl.ds(1024, 256), pl.ds(256, 64)) if part == 2 else
                    (pl.ds(part * 512, 512), pl.ds(part * 128, 128)))
        return pl.ds(pl.multiple_of(part * 512, 512), 512), pl.ds(pl.multiple_of(part * 128, 128), 128)

    def kv_copies(f, part, route, landed=False):
        k_rows, v_rows = kv_rows(part)
        source, target = (0, 0, 2)[route], (1, 2, 3)[route]
        source = target if landed else source
        dev = dev_y if route == 1 else dev_core
        return (copy(kb.at[source, f, k_rows], kb.at[target, f, k_rows],
                     kv_send.at[route, part, 0], kv_recv.at[route, part, 0], dev),
                copy(vb.at[source, f, v_rows], vb.at[target, f, v_rows],
                     kv_send.at[route, part, 1], kv_recv.at[route, part, 1], dev))

    def kv_to_y(f, part, behind=None):
        if behind is not None:
            for c in kv_copies(f, behind, 1):
                c.wait_send()
        for c in kv_copies(f, part, 1):
            c.start()

    def kv_wait(f, part, route):
        for c in kv_copies(f, part, route, landed=True):
            c.wait_recv()

    def kv_forward(f, part):
        kv_wait(f, part, 1)
        for c in kv_copies(f, part, 2):
            c.start()

    def update(qfs, h, s, values, first):
        m0 = jnp.concatenate([top[f, h] for f in qfs], axis=1) if not first else LOWEST
        m = jnp.maximum(m0, jnp.max(s, axis=0, keepdims=True))
        p = jnp.exp2(s - m).astype(jnp.bfloat16)
        term = jnp.dot(values, p, preferred_element_type=jnp.float32)
        for i, f in enumerate(qfs):
            cols = slice(i * PAD, (i + 1) * PAD)
            if first:
                acc[f, h] = term[:, cols]
            else:
                acc[f, h] = acc[f, h] * jnp.exp2(m0[:, cols] - m[:, cols]) + term[:, cols]
            top[f, h] = m[:, cols]

    def block(qfs, parts, h, first=False):
        rows = pl.ds(pl.multiple_of(h // 2 * 512, 512), 512)
        chans = pl.ds(pl.multiple_of(h * HD, HD), HD)
        keys = jnp.concatenate([kb[s, f, rows, :] for s, f in parts], axis=0)
        vals = jnp.concatenate([vb[s, f, chans, :] for s, f in parts], axis=1)
        q = jnp.concatenate([qz[f, h] for f in qfs], axis=1)
        s = jnp.dot(keys, q, preferred_element_type=jnp.float32)
        update(qfs, h, s, jnp.concatenate([vals, ones[0, :, 0:PAD * len(parts)]], axis=0), first)

    def block_last(qfs, parts, first=False):
        wide = 256 * len(parts)
        keys = jnp.concatenate([kb[s, f, 1024:1280, :] for s, f in parts], axis=0)
        vals = jnp.concatenate([vb[s, f, 256:320, 0:256] for s, f in parts]
                               + [vb[s, f, 256:320, 256:512] for s, f in parts], axis=1)
        q = [jnp.concatenate([qz[f, h] for f in qfs], axis=1) for h in (4, 5)]
        s = jnp.concatenate([jnp.dot(keys, t, preferred_element_type=jnp.float32) for t in q], axis=0)
        mask = jnp.concatenate([ones[1, :, 0:wide], ones[2, :, 0:wide]], axis=1)
        update(qfs, 4, s, jnp.concatenate([vals, mask], axis=0), first)

    def a_piece(n):
        def one(owner, part, i, dev):
            first, count = (0, HD) if part is None else (part * 32, 32)
            if not isinstance(n, int) or n < 4:
                piece = at.at[owner, :, pl.ds(pl.multiple_of(n * HD + first, 32), count)]
            else:
                piece = at.at[owner, n - 4, pl.ds(256 + first, count)]
            return copy(piece, piece, a_send.at[n, i], a_recv.at[n, i], dev)

        def begin():
            one(x, None, 0, dev_r).start()
            one(x, None, 1, dev_l).start()

        def relay():
            one(left, None, 0, dev_l).wait_recv()
            one(left, 0, 2, dev_r).start()
            one(right, None, 1, dev_r).wait_recv()
            one(right, 1, 3, dev_l).start()

        def last():
            one(far, 0, 2, dev_l).wait_recv()
            one(far, 1, 3, dev_r).wait_recv()

        def drain():
            one(x, None, 0, dev_r).wait_send()
            one(x, None, 1, dev_l).wait_send()
            one(left, 0, 2, dev_r).wait_send()
            one(right, 1, 3, dev_l).wait_send()

        return begin, relay, last, drain

    def finish(h, f):
        at[x, f, pl.ds(pl.multiple_of(h * HD, HD), HD), :] = (
            acc[f, h, 0:HD, :] / acc[f, h, HD:HD + 1, :]).astype(jnp.bfloat16)

    x_relay[0]()
    x_near[0]()
    x_last[0]()
    x_begin[1]()
    project(0)
    kv_wait(0, 3, 0)
    mine = ((0, 0), (1, 0))

    def early(h, _):
        block((0,), mine, h, True)
        return 0

    lax.fori_loop(0, 3, early, 0)
    x_relay[1]()
    lax.fori_loop(3, 4, early, 0)
    block_last((0,), mine, True)
    x_near[1]()
    x_last[1]()

    def o_copies():
        return [copy(wt.at[to], wog.at[x], o_send.at[i], o_recv.at[i], (kf, to))
                for i, to in enumerate((right, far, left))]

    for c in o_copies():
        c.start()
    project(1)

    def second(h, _):
        block((1,), mine, h, True)
        return 0

    lax.fori_loop(0, 2, second, 0)
    kv_forward(0, 3)
    lax.fori_loop(2, 4, second, 0)
    block_last((1,), mine, True)
    both = (0, 1)

    def near_block(h, _):
        block(both, ((0, 1), (1, 1), (2, 0), (3, 0)), h)
        return 0

    def far_block(h, relays):
        block(both, ((2, 1), (3, 1)), h)
        for n in relays:
            a_piece(n)[1]()
        for f in both:
            finish(h, f)
        a_piece(h)[0]()

    def first_far(h, _):
        far_block(h, ())
        return 0

    kv_wait(0, 3, 2)
    kv_wait(1, 0, 0)
    lax.fori_loop(0, 1, near_block, 0)
    kv_to_y(1, 1, 0)
    kv_forward(1, 0)
    lax.fori_loop(1, 2, near_block, 0)
    kv_to_y(1, 2, 1)
    kv_wait(1, 0, 2)
    lax.fori_loop(0, 2, first_far, 0)
    kv_wait(1, 1, 0)
    kv_forward(1, 1)

    def later(h, _):
        near_block(h, 0)

        @pl.when(h == 2)
        def _():
            a_piece(0)[1]()
            kv_wait(1, 1, 2)

        @pl.when(h == 3)
        def _():
            kv_forward(1, 2)

        far_block(h, (h - 1,))
        return 0

    lax.fori_loop(2, 4, later, 0)
    kv_wait(1, 2, 0)
    kv_wait(1, 2, 2)
    rest = ((0, 1), (1, 1), (2, 0), (3, 0), (2, 1), (3, 1))
    block_last((0,), rest)
    finish(4, 0)
    a_piece(4)[0]()
    block_last((1,), rest)
    a_piece(3)[1]()
    finish(4, 1)
    a_piece(5)[0]()

    def mix(f, first, count):
        w = jnp.concatenate([wog[g, :, first:first + count] for g in range(n_x)], axis=1)
        a = jnp.concatenate([at[g, f, first:first + count, :] for g in range(n_x)], axis=0)
        return jnp.dot(w, a, preferred_element_type=jnp.float32)

    for i, source in enumerate((left, far, right)):
        copy(wog.at[source], wog.at[source], o_send.at[i], o_recv.at[i], (kf, source)).wait_recv()
    a_piece(0)[2]()
    a_piece(1)[2]()
    total = [mix(f, 0, 128) for f in both]
    a_piece(4)[1]()
    a_piece(2)[2]()
    a_piece(5)[1]()
    a_piece(3)[2]()
    total = [total[f] + mix(f, 128, 128) for f in both]
    for f in both:
        a_piece(4 + f)[2]()
        out_ref[f] = (total[f] + mix(f, 256, 64)).astype(jnp.bfloat16)
        if f == 0:
            first_ref[0] = out_ref[0]

    for f in range(2):
        x_drain[f]()
        for part in pieces(f):
            for route in range(3):
                if route != 1 or part > 1:
                    for c in kv_copies(f, part, route):
                        c.wait_send()
    for n in range(6):
        a_piece(n)[3]()
    for c in o_copies():
        c.wait_send()


def blend(base, first_ref, second_ref, key_ref, tok_ref, num_ref, out_ref):
    each = out_ref.shape[0]
    first_key = 2 * lax.axis_index("kf") + base
    window = jnp.concatenate([first_ref[...], second_ref[...]], axis=1)
    spot = lax.broadcasted_iota(jnp.int16, (2 * PAD, TOK), 0)
    none = jnp.zeros((), jnp.bfloat16)
    for j in range(each):
        rows = ((key_ref[j] - first_key) * PAD + tok_ref[j]).astype(jnp.int16)
        share = num_ref[base * each + j:base * each + j + 1, :].astype(jnp.float32) / DEN
        pick = (jnp.where(spot == rows[0:1], share.astype(jnp.bfloat16), none)
                + jnp.where(spot == rows[1:2], (1.0 - share).astype(jnp.bfloat16), none))
        out_ref[j] = jnp.dot(window, pick, preferred_element_type=jnp.float32).astype(jnp.bfloat16)


def blend_first(ko_ref, key_ref, tok_ref, num_ref, key_out, out_ref):
    key_out[...] = ko_ref[:, :, 0:TOK]
    blend(0, ko_ref.at[0], ko_ref.at[1], key_ref, tok_ref, num_ref, out_ref)


def blend_second(ko_ref, next_ref, key_ref, tok_ref, num_ref, done_ref, out_ref):
    blend(1, ko_ref.at[1], next_ref.at[0], key_ref, tok_ref, num_ref, out_ref)


def body(key_states, w_query, w_key, w_value, w_out, gain, bias, src_key, src_tok, weight_num):
    n_x, n_kf = lax.axis_size("head"), lax.axis_size("kf")
    frames, tokens, width = key_states.shape
    full = gain.shape[0]
    vmem = pl.BlockSpec(memory_space=pltpu.VMEM)
    anywhere = pl.BlockSpec(memory_space=pltpu.HBM)
    bf16, f32 = jnp.bfloat16, jnp.float32
    dma = pltpu.SemaphoreType.DMA
    ko, ko_first = pl.pallas_call(
        functools.partial(attend, n_x),
        out_shape=(jax.ShapeDtypeStruct((2, width, PAD), bf16), jax.ShapeDtypeStruct((1, width, PAD), bf16)),
        in_specs=[anywhere] * 5 + [vmem, vmem],
        out_specs=(vmem, vmem),
        scratch_shapes=[
            pltpu.VMEM((frames, width, tokens), bf16),
            pltpu.VMEM((width, full), bf16), pltpu.VMEM((width, full), bf16), pltpu.VMEM((width, full), bf16),
            pltpu.VMEM((width, full), bf16),
            pltpu.VMEM((2, full, PAD), bf16),
            pltpu.VMEM((full, PAD), bf16),
            pltpu.VMEM((2, 6, 128, PAD), bf16),
            pltpu.VMEM((4, 2, 1280, 128), bf16),
            pltpu.VMEM((4, 2, width, PAD), bf16),
            pltpu.VMEM((3, 16, 6 * PAD), bf16),
            pltpu.VMEM((2, 5, 80, PAD), f32),
            pltpu.VMEM((2, 5, 1, PAD), f32),
            pltpu.VMEM((4, 2, width, PAD), bf16),
            pltpu.VMEM((4, width, width), bf16),
            pltpu.VMEM((4, width, width), bf16),
            pltpu.VMEM((2, full, 128), f32),
            dma((5,)), dma((2, 6)), dma((2, 6)), dma((3, 4, 2)), dma((3, 4, 2)),
            dma((6, 4)), dma((6, 4)), dma((3,)), dma((3,)),
        ],
        compiler_params=pltpu.CompilerParams(
            collective_id=0, has_side_effects=True, vmem_limit_bytes=56 * 2**20),
        name="attend",
    )(key_states.transpose(0, 2, 1), w_query.T, w_key.T, w_value.T, w_out,
      gain.reshape(full // 128, 128), bias.reshape(full // 128, 128))

    following = lax.ppermute(ko_first, "kf", [(i, i - 1) for i in range(1, n_kf)])

    def whole(shape):
        return pl.BlockSpec(shape, lambda j: (0,) * len(shape))

    n_out = weight_num.shape[0]
    each = n_out // frames
    keys_t, toks_t = src_key.transpose(0, 2, 1), src_tok.transpose(0, 2, 1)
    params = pltpu.CompilerParams(vmem_limit_bytes=40 * 2**20)
    cost = pl.CostEstimate(flops=2 * each * width * 2 * PAD * PAD, bytes_accessed=4_000_000, transcendentals=0)

    def part(base, shape):
        return pl.BlockSpec((each,) + shape, lambda j: (base, 0, 0))

    out = jax.ShapeDtypeStruct((n_out, width, tokens), bf16)
    key_out, half_done = pl.pallas_call(
        blend_first,
        grid=(1,),
        out_shape=(jax.ShapeDtypeStruct((frames, width, tokens), bf16), out),
        in_specs=[whole((2, width, PAD)), part(0, (2, tokens)), part(0, (2, tokens)), whole((n_out, tokens))],
        out_specs=(whole((frames, width, tokens)), part(0, (width, tokens))),
        compiler_params=params, cost_estimate=cost, name="blend_first",
    )(ko, keys_t, toks_t, weight_num)
    blended = pl.pallas_call(
        blend_second,
        grid=(1,),
        out_shape=out,
        in_specs=[whole((2, width, PAD)), whole((1, width, PAD)), part(1, (2, tokens)), part(1, (2, tokens)),
                  whole((n_out, tokens)), anywhere],
        out_specs=part(1, (width, tokens)),
        input_output_aliases={5: 0},
        compiler_params=params, cost_estimate=cost, name="blend_second",
    )(ko, following, keys_t, toks_t, weight_num, half_done)
    return key_out.transpose(0, 2, 1), blended.transpose(0, 2, 1)


def solution(mesh):
    return jax.shard_map(
        body,
        mesh=mesh,
        in_specs=(
            P("kf", None, "head"),
            P(None, "head"),
            P(None, "head"),
            P(None, "head"),
            P("head", None),
            P(),
            P(),
            P("kf", None, None),
            P("kf", None, None),
            P("kf", None),
        ),
        out_specs=(P("kf", None, "head"), P("kf", None, "head")),
        check_vma=False,
    )
```

time: 562 us -> 92 us (0.16)
  waiting for transfers between devices: 194 us -> 0.01 us
  local copies, waits for them, and re-layouts: 163 us -> 3.47 us
  matrix products: 124 us -> 0 us
  Pallas kernels: 0 us -> 82.5 us
  other arithmetic: 59.3 us -> 0 us
  between operations: 14.3 us -> 0.66 us
    dot_general x14 -> x0, matrix products: 124 us -> none  [the longest x5 47.7 us: head_attention(): jnp.dot(probs, value_h, preferred_element_type=jnp.float32)]
    ppermute x3 -> x1, waiting for transfers between devices: 113 us -> 0.01 us  [body(): lax.ppermute(ko_first, 'kf', [(i, i - 1) for i in range(1, n_kf)])]
    gather x6 -> x0, local copies, waits for them, and re-layouts: 89.2 us -> none  [the longest x3 44.6 us: body(): second = jnp.take(window, rows_second, axis=0).astype(jnp.float32)]
    pallas_call x0 -> x3, Pallas kernels: none -> 82.5 us  [the longest x1 74.3 us: body(): pl.pallas_call(functools.partial(attend, n_x), out_shape=(jax.ShapeDtypeS...]
    reduce_sum x7 -> x0, other arithmetic: 47.7 us -> none  [the longest x5 42.9 us: head_attention(): probs = (expo / jnp.sum(expo, axis=-1, keepdims=True)).astype(jnp.bfloat16)]
    concatenate x1 -> x0, local copies, waits for them, and re-layouts: 43.9 us -> none  [body(): batch_normed = jnp.concatenate([batch_normed, mates], axis=0)]
    all_gather x1 -> x0, waiting for transfers between devices: 43.4 us -> none  [body(): full = lax.all_gather(key_states, 'head', axis=2, tiled=True)]
    reduce_scatter x1 -> x0, waiting for transfers between devices: 37 us -> none  [body(): lax.psum_scatter(terms.astype(jnp.bfloat16), 'head', scatter_dimension=1,...]
  transfers between devices with their start and end apart: 5 -> 1, of which waited for: 5 -> 0; matrix products, arithmetic and copies ran while one was open for 2% -> 0% of each run, Pallas kernels for 0% -> 5%
where the time goes in v2:
time: 92 us; the launch traced here: 91.7 us
  Pallas kernels  82.5 us (90%)
  starting transfers between devices  5.03 us (5%)
  local copies, waits for them, and re-layouts  3.47 us (4%)
    pallas_call x1, Pallas kernels, body(): pl.pallas_call(functools.partial(attend, n_x), out_shape=(jax.ShapeDtypeS...  74.3 us
    ppermute x1, starting transfers between devices, body(): lax.ppermute(ko_first, 'kf', [(i, i - 1) for i in range(1, n_kf)])  5.03 us
    pallas_call x1, Pallas kernels, body(): pl.pallas_call(blend_first, grid=(1,), out_shape=(jax.ShapeDtypeStruct((f...  4.18 us
    pallas_call x1, Pallas kernels, body(): pl.pallas_call(blend_second, grid=(1,), out_shape=out, in_specs=[whole((2...  3.99 us
    unnamed x8, local copies, waits for them, and re-layouts  3.47 us
  transfers between devices with their start and end apart: 1, of which 0 were waited for; matrix products, arithmetic and copies ran while one was open for 0% of the time, Pallas kernels for 5%

profile of v2, /device:TPU:1, one launch (start us, length us, event | category | flops | bytes accessed | tf_op | source)
XLA Modules:
  0.0 91.7 jit_solution(8097789529047882411)
XLA Ops:
  0.6 74.3 %attend.1 = (bf16[2,320,512]{2,1,0:T(8,128)(2,1)}, bf16[1,320,512]{2,1,0:T(8,128)(2,1)}) custom-call(bf16[2,320,510]{2,1,0:T(8,128)(2,1)} %bitcast.18, bf16[320,1280]{1,0:T(8,128)(2,1)} %bitcast.15, bf16[320,1280]{1,0:T(8,128)(2,1)} %bitcast.16, bf16[320,1280]{1,0:T(8,128)(2,1)} %bitcast.17, bf16[320,1280]{1,0:T(8,128)(2,1)} %wo_hbm.1, f32[10,128]{1,0:T(8,128)} %bitcast.19, ...), custom_call_target="tpu_custom_call" | custom-call | tf_op jit(solution)/shard_map/attend/pallas_call | solution.py:399
  75.0 5.0 %collective-permute-start = (bf16[1,320,512]{2,1,0:T(8,128)(2,1)}, bf16[1,320,512]{2,1,0:T(8,128)(2,1)S(1)}, u32[]{:S(2)}, u32[]{:S(2)}) collective-permute-start(bf16[1,320,512]{2,1,0:T(8,128)(2,1)} %get-tuple-element.8), channel_id=1, source_target_pairs={{4,0},{8,4},{12,8},{16,12},{20,16},{24,20},{28,24},{32,28},{36,32}... | collective-permute-start | bytes 983048 | tf_op jit(solution)/shard_map/ppermute | solution.py:429
  80.0 0.0 copy-start
  80.0 1.1 %copy-done = bf16[2,320,512]{2,1,0:T(8,128)(2,1)S(1)} copy-done((bf16[2,320,512]{2,1,0:T(8,128)(2,1)S(1)}, bf16[2,320,512]{2,1,0:T(8,128)(2,1)}, u32[]{:S(2)}) %copy-start) | copy-done | bytes 655384
  81.1 0.0 copy-start.1
  81.1 0.8 copy-done.1
  81.9 0.0 copy-start.2
  81.9 0.8 copy-done.2
  82.7 0.0 copy-start.3
  82.7 0.8 copy-done.3
  83.5 4.2 %blend_first.1 = (bf16[2,320,510]{2,1,0:T(8,128)(2,1)}, bf16[14,320,510]{2,1,0:T(8,128)(2,1)}) custom-call(bf16[2,320,512]{2,1,0:T(8,128)(2,1)S(1)} %copy-done, s32[14,2,510]{2,1,0:T(2,128)S(1)} %bitcast.10, s32[14,2,510]{2,1,0:T(2,128)S(1)} %bitcast.12, s32[14,510]{1,0:T(8,128)S(1)} %copy-done.3), custom_call_target="tpu_custom_call" | custom-call | flops 2348810240 | bytes 4000000 | tf_op jit(solution)/shard_map/blend_first/pallas_call | solution.py:444
  87.7 0.0 collective-permute-done.next_ref
  87.7 4.0 %blend_second.1 = bf16[14,320,510]{2,1,0:T(8,128)(2,1)} custom-call(bf16[2,320,512]{2,1,0:T(8,128)(2,1)S(1)} %copy-done, bf16[1,320,512]{2,1,0:T(8,128)(2,1)S(1)} %collective-permute-done.next_ref, s32[14,2,510]{2,1,0:T(2,128)S(1)} %bitcast.11, s32[14,2,510]{2,1,0:T(2,128)S(1)} %bitcast.13, s32[14,510]{1,0:T(8,128)S(1)} %copy-done.3, ...), custom_call_target="tpu_custom_call", output_to_operand_aliasing={{}: (5, {})} | custom-call | flops 2348810240 | bytes 4000000 | tf_op jit(solution)/shard_map/blend_second/pallas_call | solution.py:452
Async XLA Ops:
  75.0 12.7 %collective-permute-start = (bf16[1,320,512]{2,1,0:T(8,128)(2,1)}, bf16[1,320,512]{2,1,0:T(8,128)(2,1)S(1)}, u32[]{:S(2)}, u32[]{:S(2)}) collective-permute-start(bf16[1,320,512]{2,1,0:T(8,128)(2,1)} %get-tuple-element.8), channel_id=1, source_target_pairs={{4,0},{8,4},{12,8},{16,12},{20,16},{24,20},{28,24},{32,28},{36,32}... | collective-permute-start | bytes 983048 | tf_op jit(solution)/shard_map/ppermute | solution.py:429
  80.0 1.1 %copy-start = (bf16[2,320,512]{2,1,0:T(8,128)(2,1)S(1)}, bf16[2,320,512]{2,1,0:T(8,128)(2,1)}, u32[]{:S(2)}) copy-start(bf16[2,320,512]{2,1,0:T(8,128)(2,1)} %get-tuple-element.6.ko_ref) | copy-start | bytes 1966084
  81.1 0.8 copy-start.1
  81.9 0.8 copy-start.2
  82.7 0.8 copy-start.3

commit v3 on v2

--- a/solution.py
+++ b/solution.py
@@ -46,10 +46,18 @@
         def one(owner, part, i, dev):
             return copy(piece(owner, part), piece(owner, part), sends(i), recvs(i), dev)
 
-        def begin():
-            for part, i in ((0, 0), (1, 1)):
-                one(x, part, i, dev_r).start()
-                one(x, 1 - part, 2 + i, dev_l).start()
+        def begin(halves=(0, 1)):
+            for i in halves:
+                one(x, i, i, dev_r).start()
+                one(x, 1 - i, 2 + i, dev_l).start()
+
+        def sent(i):
+            if i < 2:
+                one(x, i, i, dev_r).wait_send()
+                one(x, 1 - i, 2 + i, dev_l).wait_send()
+            else:
+                one(left, 0, 4, dev_r).wait_send()
+                one(right, 1, 5, dev_l).wait_send()
 
         def relay():
             one(left, 0, 0, dev_l).wait_recv()
@@ -65,14 +73,7 @@
             one(far, 0, 4, dev_l).wait_recv()
             one(far, 1, 5, dev_r).wait_recv()
 
-        def drain():
-            for part, i in ((0, 0), (1, 1)):
-                one(x, part, i, dev_r).wait_send()
-                one(x, 1 - part, 2 + i, dev_l).wait_send()
-            one(left, 0, 4, dev_r).wait_send()
-            one(right, 1, 5, dev_l).wait_send()
-
-        return begin, relay, near, last, drain
+        return begin, relay, near, last, sent
 
     def x_piece(f):
         def piece(owner, part):
@@ -80,7 +81,7 @@
 
         return ring(piece, lambda i: x_send.at[f, i], lambda i: x_recv.at[f, i])
 
-    x_begin, x_relay, x_near, x_last, x_drain = zip(x_piece(0), x_piece(1))
+    x_begin, x_relay, x_near, x_last, x_sent = zip(x_piece(0), x_piece(1))
 
     loads[0].wait()
     own_rows = pl.ds(pl.multiple_of(x * width, 64), width)
@@ -156,10 +157,7 @@
                 copy(vb.at[source, f, v_rows], vb.at[target, f, v_rows],
                      kv_send.at[route, part, 1], kv_recv.at[route, part, 1], dev))
 
-    def kv_to_y(f, part, behind=None):
-        if behind is not None:
-            for c in kv_copies(f, behind, 1):
-                c.wait_send()
+    def kv_to_y(f, part):
         for c in kv_copies(f, part, 1):
             c.start()
 
@@ -241,8 +239,9 @@
 
     x_relay[0]()
     x_near[0]()
+    x_sent[0](2)
+    x_begin[1]()
     x_last[0]()
-    x_begin[1]()
     project(0)
     kv_wait(0, 3, 0)
     mine = ((0, 0), (1, 0))
@@ -271,6 +270,7 @@
         return 0
 
     lax.fori_loop(0, 2, second, 0)
+    kv_to_y(1, 1)
     kv_forward(0, 3)
     lax.fori_loop(2, 4, second, 0)
     block_last((1,), mine, True)
@@ -295,10 +295,9 @@
     kv_wait(0, 3, 2)
     kv_wait(1, 0, 0)
     lax.fori_loop(0, 1, near_block, 0)
-    kv_to_y(1, 1, 0)
+    kv_to_y(1, 2)
     kv_forward(1, 0)
     lax.fori_loop(1, 2, near_block, 0)
-    kv_to_y(1, 2, 1)
     kv_wait(1, 0, 2)
     lax.fori_loop(0, 2, first_far, 0)
     kv_wait(1, 1, 0)
@@ -353,39 +352,43 @@
             first_ref[0] = out_ref[0]
 
     for f in range(2):
-        x_drain[f]()
+        for i in ((0, 1), (0, 1, 2))[f]:
+            x_sent[f](i)
         for part in pieces(f):
             for route in range(3):
-                if route != 1 or part > 1:
-                    for c in kv_copies(f, part, route):
-                        c.wait_send()
+                for c in kv_copies(f, part, route):
+                    c.wait_send()
     for n in range(6):
         a_piece(n)[3]()
     for c in o_copies():
         c.wait_send()
 
 
-def blend(base, first_ref, second_ref, key_ref, tok_ref, num_ref, out_ref):
-    each = out_ref.shape[0]
+def blend(base, first_ref, second_ref, key_ref, tok_ref, num_ref, out_hbm, made, sems):
+    each = made.shape[0]
     first_key = 2 * lax.axis_index("kf") + base
     window = jnp.concatenate([first_ref[...], second_ref[...]], axis=1)
     spot = lax.broadcasted_iota(jnp.int16, (2 * PAD, TOK), 0)
     none = jnp.zeros((), jnp.bfloat16)
+    copies = [pltpu.make_async_copy(made.at[j], out_hbm.at[base * each + j], sems.at[j]) for j in range(each)]
     for j in range(each):
         rows = ((key_ref[j] - first_key) * PAD + tok_ref[j]).astype(jnp.int16)
         share = num_ref[base * each + j:base * each + j + 1, :].astype(jnp.float32) / DEN
         pick = (jnp.where(spot == rows[0:1], share.astype(jnp.bfloat16), none)
                 + jnp.where(spot == rows[1:2], (1.0 - share).astype(jnp.bfloat16), none))
-        out_ref[j] = jnp.dot(window, pick, preferred_element_type=jnp.float32).astype(jnp.bfloat16)
-
-
-def blend_first(ko_ref, key_ref, tok_ref, num_ref, key_out, out_ref):
+        made[j] = jnp.dot(window, pick, preferred_element_type=jnp.float32).astype(jnp.bfloat16)
+        copies[j].start()
+    for c in copies:
+        c.wait()
+
+
+def blend_first(ko_ref, key_ref, tok_ref, num_ref, key_out, out_hbm, made, sems):
     key_out[...] = ko_ref[:, :, 0:TOK]
-    blend(0, ko_ref.at[0], ko_ref.at[1], key_ref, tok_ref, num_ref, out_ref)
-
-
-def blend_second(ko_ref, next_ref, key_ref, tok_ref, num_ref, done_ref, out_ref):
-    blend(1, ko_ref.at[1], next_ref.at[0], key_ref, tok_ref, num_ref, out_ref)
+    blend(0, ko_ref.at[0], ko_ref.at[1], key_ref, tok_ref, num_ref, out_hbm, made, sems)
+
+
+def blend_second(ko_ref, next_ref, key_ref, tok_ref, num_ref, done_ref, out_hbm, made, sems):
+    blend(1, ko_ref.at[1], next_ref.at[0], key_ref, tok_ref, num_ref, out_hbm, made, sems)
 
 
 def body(key_states, w_query, w_key, w_value, w_out, gain, bias, src_key, src_tok, weight_num):
@@ -441,12 +444,14 @@
         return pl.BlockSpec((each,) + shape, lambda j: (base, 0, 0))
 
     out = jax.ShapeDtypeStruct((n_out, width, tokens), bf16)
+    made = [pltpu.VMEM((each, width, tokens), bf16), dma((each,))]
     key_out, half_done = pl.pallas_call(
         blend_first,
         grid=(1,),
         out_shape=(jax.ShapeDtypeStruct((frames, width, tokens), bf16), out),
         in_specs=[whole((2, width, PAD)), part(0, (2, tokens)), part(0, (2, tokens)), whole((n_out, tokens))],
-        out_specs=(whole((frames, width, tokens)), part(0, (width, tokens))),
+        out_specs=(whole((frames, width, tokens)), anywhere),
+        scratch_shapes=made,
         compiler_params=params, cost_estimate=cost, name="blend_first",
     )(ko, keys_t, toks_t, weight_num)
     blended = pl.pallas_call(
@@ -455,7 +460,8 @@
         out_shape=out,
         in_specs=[whole((2, width, PAD)), whole((1, width, PAD)), part(1, (2, tokens)), part(1, (2, tokens)),
                   whole((n_out, tokens)), anywhere],
-        out_specs=part(1, (width, tokens)),
+        out_specs=anywhere,
+        scratch_shapes=made,
         input_output_aliases={5: 0},
         compiler_params=params, cost_estimate=cost, name="blend_second",
     )(ko, following, keys_t, toks_t, weight_num, half_done)

time: 92 us -> 89.6 us (0.974)
  Pallas kernels: 82.5 us -> 79.8 us
    pallas_call x1, Pallas kernels: 74.3 us -> 72.2 us  [body(): pl.pallas_call(functools.partial(attend, n_x), out_shape=(jax.ShapeDtypeS...]
where the time goes in v3:
time: 89.6 us; the launch traced here: 89.2 us
  Pallas kernels  79.8 us (89%)
  starting transfers between devices  5.04 us (6%)
  local copies, waits for them, and re-layouts  3.47 us (4%)
    pallas_call x1, Pallas kernels, body(): pl.pallas_call(functools.partial(attend, n_x), out_shape=(jax.ShapeDtypeS...  72.2 us
    ppermute x1, starting transfers between devices, body(): lax.ppermute(ko_first, 'kf', [(i, i - 1) for i in range(1, n_kf)])  5.04 us
    pallas_call x1, Pallas kernels, body(): pl.pallas_call(blend_first, grid=(1,), out_shape=(jax.ShapeDtypeStruct((f...  4.25 us
    unnamed x8, local copies, waits for them, and re-layouts  3.47 us
    pallas_call x1, Pallas kernels, body(): pl.pallas_call(blend_second, grid=(1,), out_shape=out, in_specs=[whole((2...  3.4 us
  transfers between devices with their start and end apart: 1, of which 0 were waited for; matrix products, arithmetic and copies ran while one was open for 0% of the time, Pallas kernels for 5%

profile of v3, /device:TPU:1, one launch (start us, length us, event | category | flops | bytes accessed | tf_op | source)
XLA Modules:
  0.0 89.2 jit_solution(8863171946484318968)
XLA Ops:
  0.6 72.2 %attend.1 = (bf16[2,320,512]{2,1,0:T(8,128)(2,1)}, bf16[1,320,512]{2,1,0:T(8,128)(2,1)}) custom-call(bf16[2,320,510]{2,1,0:T(8,128)(2,1)} %bitcast.18, bf16[320,1280]{1,0:T(8,128)(2,1)} %bitcast.15, bf16[320,1280]{1,0:T(8,128)(2,1)} %bitcast.16, bf16[320,1280]{1,0:T(8,128)(2,1)} %bitcast.17, bf16[320,1280]{1,0:T(8,128)(2,1)} %wo_hbm.1, f32[10,128]{1,0:T(8,128)} %bitcast.19, ...), custom_call_target="tpu_custom_call" | custom-call | tf_op jit(solution)/shard_map/attend/pallas_call | solution.py:402
  72.8 5.0 %collective-permute-start = (bf16[1,320,512]{2,1,0:T(8,128)(2,1)}, bf16[1,320,512]{2,1,0:T(8,128)(2,1)S(1)}, u32[]{:S(2)}, u32[]{:S(2)}) collective-permute-start(bf16[1,320,512]{2,1,0:T(8,128)(2,1)} %get-tuple-element.8), channel_id=1, source_target_pairs={{4,0},{8,4},{12,8},{16,12},{20,16},{24,20},{28,24},{32,28},{36,32}... | collective-permute-start | bytes 983048 | tf_op jit(solution)/shard_map/ppermute | solution.py:432
  77.8 0.0 copy-start
  77.9 1.1 %copy-done = bf16[2,320,512]{2,1,0:T(8,128)(2,1)S(1)} copy-done((bf16[2,320,512]{2,1,0:T(8,128)(2,1)S(1)}, bf16[2,320,512]{2,1,0:T(8,128)(2,1)}, u32[]{:S(2)}) %copy-start) | copy-done | bytes 655384
  78.9 0.0 copy-start.1
  78.9 0.8 copy-done.1
  79.8 0.0 copy-start.2
  79.8 0.8 copy-done.2
  80.6 0.0 copy-start.3
  80.6 0.8 copy-done.3
  81.3 4.3 %blend_first.1 = (bf16[2,320,510]{2,1,0:T(8,128)(2,1)}, bf16[14,320,510]{2,1,0:T(8,128)(2,1)}) custom-call(bf16[2,320,512]{2,1,0:T(8,128)(2,1)S(1)} %copy-done, s32[14,2,510]{2,1,0:T(2,128)S(1)} %bitcast.10, s32[14,2,510]{2,1,0:T(2,128)S(1)} %bitcast.12, s32[14,510]{1,0:T(8,128)S(1)} %copy-done.3), custom_call_target="tpu_custom_call" | custom-call | flops 2348810240 | bytes 4000000 | tf_op jit(solution)/shard_map/blend_first/pallas_call | solution.py:448
  85.6 0.0 collective-permute-done.next_ref
  85.6 3.4 %blend_second.1 = bf16[14,320,510]{2,1,0:T(8,128)(2,1)} custom-call(bf16[2,320,512]{2,1,0:T(8,128)(2,1)S(1)} %copy-done, bf16[1,320,512]{2,1,0:T(8,128)(2,1)S(1)} %collective-permute-done.next_ref, s32[14,2,510]{2,1,0:T(2,128)S(1)} %bitcast.11, s32[14,2,510]{2,1,0:T(2,128)S(1)} %bitcast.13, s32[14,510]{1,0:T(8,128)S(1)} %copy-done.3, ...), custom_call_target="tpu_custom_call", output_to_operand_aliasing={{}: (5, {})} | custom-call | flops 2348810240 | bytes 4000000 | tf_op jit(solution)/shard_map/blend_second/pallas_call | solution.py:457
Async XLA Ops:
  72.8 12.8 %collective-permute-start = (bf16[1,320,512]{2,1,0:T(8,128)(2,1)}, bf16[1,320,512]{2,1,0:T(8,128)(2,1)S(1)}, u32[]{:S(2)}, u32[]{:S(2)}) collective-permute-start(bf16[1,320,512]{2,1,0:T(8,128)(2,1)} %get-tuple-element.8), channel_id=1, source_target_pairs={{4,0},{8,4},{12,8},{16,12},{20,16},{24,20},{28,24},{32,28},{36,32}... | collective-permute-start | bytes 983048 | tf_op jit(solution)/shard_map/ppermute | solution.py:432
  77.8 1.1 %copy-start = (bf16[2,320,512]{2,1,0:T(8,128)(2,1)S(1)}, bf16[2,320,512]{2,1,0:T(8,128)(2,1)}, u32[]{:S(2)}) copy-start(bf16[2,320,512]{2,1,0:T(8,128)(2,1)} %get-tuple-element.6.ko_ref) | copy-start | bytes 1966084
  78.9 0.8 copy-start.1
  79.8 0.8 copy-start.2
  80.6 0.8 copy-start.3

commit v4 on v3

--- a/solution.py
+++ b/solution.py
@@ -382,9 +382,12 @@
         c.wait()
 
 
-def blend_first(ko_ref, key_ref, tok_ref, num_ref, key_out, out_hbm, made, sems):
-    key_out[...] = ko_ref[:, :, 0:TOK]
+def blend_first(ko_ref, key_ref, tok_ref, num_ref, key_out, out_hbm, made, sems, cut, cut_sem):
+    cut[...] = ko_ref[:, :, 0:TOK]
+    leave = pltpu.make_async_copy(cut, key_out, cut_sem)
+    leave.start()
     blend(0, ko_ref.at[0], ko_ref.at[1], key_ref, tok_ref, num_ref, out_hbm, made, sems)
+    leave.wait()
 
 
 def blend_second(ko_ref, next_ref, key_ref, tok_ref, num_ref, done_ref, out_hbm, made, sems):
@@ -450,8 +453,8 @@
         grid=(1,),
         out_shape=(jax.ShapeDtypeStruct((frames, width, tokens), bf16), out),
         in_specs=[whole((2, width, PAD)), part(0, (2, tokens)), part(0, (2, tokens)), whole((n_out, tokens))],
-        out_specs=(whole((frames, width, tokens)), anywhere),
-        scratch_shapes=made,
+        out_specs=(anywhere, anywhere),
+        scratch_shapes=made + [pltpu.VMEM((frames, width, tokens), bf16), dma],
         compiler_params=params, cost_estimate=cost, name="blend_first",
     )(ko, keys_t, toks_t, weight_num)
     blended = pl.pallas_call(

time: 89.6 us -> 88.9 us (level)
  transfers between devices with their start and end apart: 1 -> 1, of which waited for: 0 -> 0; matrix products, arithmetic and copies ran while one was open for 0% -> 0% of each run, Pallas kernels for 5% -> 4%
where the time goes in v4:
time: 88.9 us; the launch traced here: 88.5 us
  Pallas kernels  79.2 us (89%)
  starting transfers between devices  5.04 us (6%)
  local copies, waits for them, and re-layouts  3.47 us (4%)
    pallas_call x1, Pallas kernels, body(): pl.pallas_call(functools.partial(attend, n_x), out_shape=(jax.ShapeDtypeS...  72.2 us
    ppermute x1, starting transfers between devices, body(): lax.ppermute(ko_first, 'kf', [(i, i - 1) for i in range(1, n_kf)])  5.04 us
    pallas_call x1, Pallas kernels, body(): pl.pallas_call(blend_first, grid=(1,), out_shape=(jax.ShapeDtypeStruct((f...  3.59 us
    unnamed x8, local copies, waits for them, and re-layouts  3.47 us
    pallas_call x1, Pallas kernels, body(): pl.pallas_call(blend_second, grid=(1,), out_shape=out, in_specs=[whole((2...  3.41 us
  transfers between devices with their start and end apart: 1, of which 0 were waited for; matrix products, arithmetic and copies ran while one was open for 0% of the time, Pallas kernels for 4%

profile of v4, /device:TPU:1, one launch (start us, length us, event | category | flops | bytes accessed | tf_op | source)
XLA Modules:
  0.0 88.5 jit_solution(7363353791457926483)
XLA Ops:
  0.6 72.2 %attend.1 = (bf16[2,320,512]{2,1,0:T(8,128)(2,1)}, bf16[1,320,512]{2,1,0:T(8,128)(2,1)}) custom-call(bf16[2,320,510]{2,1,0:T(8,128)(2,1)} %bitcast.18, bf16[320,1280]{1,0:T(8,128)(2,1)} %bitcast.15, bf16[320,1280]{1,0:T(8,128)(2,1)} %bitcast.16, bf16[320,1280]{1,0:T(8,128)(2,1)} %bitcast.17, bf16[320,1280]{1,0:T(8,128)(2,1)} %wo_hbm.1, f32[10,128]{1,0:T(8,128)} %bitcast.19, ...), custom_call_target="tpu_custom_call" | custom-call | tf_op jit(solution)/shard_map/attend/pallas_call | solution.py:405
  72.8 5.0 %collective-permute-start = (bf16[1,320,512]{2,1,0:T(8,128)(2,1)}, bf16[1,320,512]{2,1,0:T(8,128)(2,1)S(1)}, u32[]{:S(2)}, u32[]{:S(2)}) collective-permute-start(bf16[1,320,512]{2,1,0:T(8,128)(2,1)} %get-tuple-element.8), channel_id=1, source_target_pairs={{4,0},{8,4},{12,8},{16,12},{20,16},{24,20},{28,24},{32,28},{36,32}... | collective-permute-start | bytes 983048 | tf_op jit(solution)/shard_map/ppermute | solution.py:435
  77.8 0.0 copy-start
  77.9 1.1 %copy-done = bf16[2,320,512]{2,1,0:T(8,128)(2,1)S(1)} copy-done((bf16[2,320,512]{2,1,0:T(8,128)(2,1)S(1)}, bf16[2,320,512]{2,1,0:T(8,128)(2,1)}, u32[]{:S(2)}) %copy-start) | copy-done | bytes 655384
  78.9 0.0 copy-start.1
  78.9 0.8 copy-done.1
  79.8 0.0 copy-start.2
  79.8 0.8 copy-done.2
  80.6 0.0 copy-start.3
  80.6 0.8 copy-done.3
  81.3 3.6 %blend_first.1 = (bf16[2,320,510]{2,1,0:T(8,128)(2,1)}, bf16[14,320,510]{2,1,0:T(8,128)(2,1)}) custom-call(bf16[2,320,512]{2,1,0:T(8,128)(2,1)S(1)} %copy-done, s32[14,2,510]{2,1,0:T(2,128)S(1)} %bitcast.10, s32[14,2,510]{2,1,0:T(2,128)S(1)} %bitcast.12, s32[14,510]{1,0:T(8,128)S(1)} %copy-done.3), custom_call_target="tpu_custom_call" | custom-call | flops 2348810240 | bytes 4000000 | tf_op jit(solution)/shard_map/blend_first/pallas_call | solution.py:451
  84.9 0.0 collective-permute-done.next_ref
  84.9 3.4 %blend_second.1 = bf16[14,320,510]{2,1,0:T(8,128)(2,1)} custom-call(bf16[2,320,512]{2,1,0:T(8,128)(2,1)S(1)} %copy-done, bf16[1,320,512]{2,1,0:T(8,128)(2,1)S(1)} %collective-permute-done.next_ref, s32[14,2,510]{2,1,0:T(2,128)S(1)} %bitcast.11, s32[14,2,510]{2,1,0:T(2,128)S(1)} %bitcast.13, s32[14,510]{1,0:T(8,128)S(1)} %copy-done.3, ...), custom_call_target="tpu_custom_call", output_to_operand_aliasing={{}: (5, {})} | custom-call | flops 2348810240 | bytes 4000000 | tf_op jit(solution)/shard_map/blend_second/pallas_call | solution.py:460
Async XLA Ops:
  72.8 12.1 %collective-permute-start = (bf16[1,320,512]{2,1,0:T(8,128)(2,1)}, bf16[1,320,512]{2,1,0:T(8,128)(2,1)S(1)}, u32[]{:S(2)}, u32[]{:S(2)}) collective-permute-start(bf16[1,320,512]{2,1,0:T(8,128)(2,1)} %get-tuple-element.8), channel_id=1, source_target_pairs={{4,0},{8,4},{12,8},{16,12},{20,16},{24,20},{28,24},{32,28},{36,32}... | collective-permute-start | bytes 983048 | tf_op jit(solution)/shard_map/ppermute | solution.py:435
  77.8 1.1 %copy-start = (bf16[2,320,512]{2,1,0:T(8,128)(2,1)S(1)}, bf16[2,320,512]{2,1,0:T(8,128)(2,1)}, u32[]{:S(2)}) copy-start(bf16[2,320,512]{2,1,0:T(8,128)(2,1)} %get-tuple-element.6.ko_ref) | copy-start | bytes 1966084
  78.9 0.8 copy-start.1
  79.8 0.8 copy-start.2
  80.6 0.8 copy-start.3
